TPU v7x, 32 devices: a whole 2x2x4 slice. The times are simulated.
32 devices in a mesh: gx: 8 (over z, core), fam: 4 (over y, x).
Axes of the slice: x: 2, y: 2, z: 4, core: 2. Of those that a mesh axis runs over, the one named last changes fastest.
Arguments:
- labels: int32 [1, 512, 512], P(None, 'gx'), may hold values from 0 to 2047, as said below
- family_of_grain: int32 [2048], replicated, may hold values from 0 to 255
Outputs:
- distance: float32 [256, 1, 512, 512], P('fam', None, 'gx')
Inputs may be any that keep to these rules, and one draw needn't show every extreme that they name: `labels`: cells lie mostly in square grains of 32 x 32 cells; about a quarter of the cells carry some other grain.
All inputs are finite; a program needn't handle non-finite values.
Results may differ from a plain program's by a relative error of at most 0.0019.
Values may be sent and summed in bfloat16 or wider, within the bound.
A program may use at most 128 MiB of HBM per device.

v0:
```python
import jax
import jax.numpy as jnp
from jax import lax
from jax.sharding import PartitionSpec as P

F = 256
NX = 512
NY = 512
WIDTH = 2
SWEEPS = 3


fidelity = 0.25
scale_factor = 8.0
step_size = 0.5


def merged(value, axis, join):
    pieces = jax.tree.map(lambda part: lax.all_gather(part, axis), value)
    head = jax.tree.map(lambda part: part[0], pieces)
    tail = jax.tree.map(lambda part: part[1:], pieces)
    subtotal, _ = lax.scan(lambda subtotal, slab: (join(subtotal, slab), None), head, tail)
    return subtotal


def extended(array, sides, width):
    for axis, dim in sides:
        size, length = (lax.axis_size(axis), array.shape[dim])
        up = [(i, (i + 1) % size) for i in range(size)]
        down = [(j, i) for i, j in up]
        last = lax.slice_in_dim(array, length - width, length, axis=dim)
        initial = lax.slice_in_dim(array, 0, width, axis=dim)
        before = lax.ppermute(last, axis, up)
        after = lax.ppermute(initial, axis, down)
        array = jnp.concatenate([before, array, after], axis=dim)
    return array


def cas_table(count):
    idx = jnp.arange(count).astype(jnp.float32)
    angle = 2.0 * jnp.pi * jnp.outer(idx, idx) / count
    return (jnp.cos(angle) + jnp.sin(angle)).astype(jnp.bfloat16)


def gauss_table(count):
    freq = jnp.arange(count)
    mirror = jnp.minimum(freq, count - freq).astype(jnp.float32)
    sigma = WIDTH / 2.0
    return jnp.exp(-2.0 * jnp.pi**2 * sigma**2 * mirror**2 / (count * count))


def godunov(ext, sign):
    centre = ext[:, :, 1:-1]
    pairs = [
        (centre - ext[:, :, :-2], ext[:, :, 2:] - centre),
        (centre - jnp.roll(centre, 1, 3), jnp.roll(centre, -1, 3) - centre),
        (centre - jnp.roll(centre, 1, 1), jnp.roll(centre, -1, 1) - centre),
    ]
    plus = jnp.zeros_like(centre)
    minus = jnp.zeros_like(centre)
    for back, fore in pairs:
        plus = plus + jnp.maximum(jnp.maximum(back, 0.0) ** 2, jnp.minimum(fore, 0.0) ** 2)
        minus = minus + jnp.maximum(jnp.minimum(back, 0.0) ** 2, jnp.maximum(fore, 0.0) ** 2)
    grad = jnp.sqrt(jnp.where(sign > 0, plus, minus))
    return centre - step_size * sign * (grad - 1.0)


def pair_combine(left, right):
    high = jnp.maximum(left[0], right[0])
    second = jnp.maximum(jnp.minimum(left[0], right[0]), jnp.maximum(left[1], right[1]))
    return (high, second)


def body(labels, family_of_grain):
    fam_local = F // lax.axis_size("fam")
    first = lax.axis_index("fam") * fam_local
    owner = jnp.take(family_of_grain, labels, axis=0)
    ids = first + jnp.arange(fam_local)
    chi = (owner[None] == ids[:, None, None, None]).astype(jnp.bfloat16)
    cas_x = cas_table(NX)
    cas_y = cas_table(NY)
    gauss_x = gauss_table(NX)
    gauss_y = gauss_table(NY)
    spec_y = (
        jnp.einsum("fzxy,yk->fzxk", chi, cas_y, preferred_element_type=jnp.float32) * gauss_y
    ).astype(jnp.bfloat16)
    spec_xy = (
        jnp.einsum(
            "fzxk,xq->fzqk",
            lax.all_to_all(spec_y, "gx", split_axis=3, concat_axis=2, tiled=True),
            cas_x,
            preferred_element_type=jnp.float32,
        )
        * gauss_x[None, None, :, None]
    ).astype(jnp.bfloat16)
    lines_done = (
        jnp.einsum("fzqk,qx->fzxk", spec_xy, cas_x, preferred_element_type=jnp.float32) * (1.0 / NX)
    ).astype(jnp.bfloat16)
    back_x = lax.all_to_all(lines_done, "gx", split_axis=2, concat_axis=3, tiled=True)
    smooth = jnp.einsum("fzxk,ky->fzxy", back_x, cas_y, preferred_element_type=jnp.float32) * (
        1.0 / NY
    )
    u = smooth + fidelity * chi.astype(jnp.float32)
    ordered = jnp.sort(u, axis=0)
    top1, top2 = merged((ordered[-1], ordered[-2]), "fam", pair_combine)
    phi0 = scale_factor * (u - jnp.where(u >= top1, top2, top1))
    ext = extended(phi0, (("gx", 2),), 3)
    sign_ext = ext / jnp.sqrt(ext * ext + 1.0)
    length = ext.shape[2]
    for sweep in range(SWEEPS):
        inner = sweep + 1
        ext = godunov(ext, sign_ext[:, :, inner : length - inner])
    return ext


def solution(mesh):
    placed = (P(None, "gx", None), P())
    return jax.shard_map(
        body, mesh=mesh, in_specs=placed, out_specs=P("fam", None, "gx", None), check_vma=False
    )
```

profile of v0, /device:TPU:0, one launch (start us, length us, event | category | flops | bytes accessed | tf_op | source)
XLA Modules:
  0.0 852.9 jit_solution(5568579552573075959)
XLA Ops:
  0.0 0.0 copy-start
  0.0 0.9 fusion.15
  1.0 0.0 copy-done
  1.0 0.0 copy-start.3
  1.0 180.5 %gather_fusion = s32[32768]{0:T(1024)S(1)} fusion(s32[2048]{0:T(1024)S(1)} %copy-done, s32[32768]{0:T(1024)S(1)} %broadcast_clamp_fusion), kind=kCustom, calls=%fused_computation | custom fusion | bytes 393216 | tf_op jit(solution)/shard_map/jit(_take)/gather | solution.py:77
  181.6 0.0 copy-done.3
  181.7 8.6 %fusion.4 = bf16[64,1,64,512]{3,2,0,1:T(8,128)(2,1)} fusion(f32[512]{0:T(512)S(1)} %fusion.19, s32[64,512]{1,0:T(8,128)S(1)} %select_bitcast_fusion, s32[64]{0:T(128)S(1)} %iota_add_fusion, f32[512]{0:T(512)S(1)} %iota_convert_fusion), kind=kOutput, calls=%fused_computation.33 | convolution fusion | flops 2154823680 | bytes 4329728 | tf_op jit(solution)/shard_map/fzxy,yk->fzxk/dot_general | solution.py:85
  190.3 12.9 %copy.14 = bf16[64,1,64,512]{2,0,1,3:T(8,128)(2,1)} copy(bf16[64,1,64,512]{3,2,0,1:T(8,128)(2,1)} %fusion.4) | data formatting | bytes 8388608 | tf_op jit(solution)/shard_map/convert_element_type | solution.py:86
  203.2 10.5 %reshape.205 = bf16[8,2,131072]{2,1,0:T(2,128)(2,1)} reshape(bf16[512,1,64,64]{3,2,1,0:T(8,128)(2,1)} %bitcast.82) | data formatting | bytes 8388608
  213.7 100.8 %all_to_all.30 = bf16[8,2,131072]{2,1,0:T(2,128)(2,1)} all-to-all(bf16[8,2,131072]{2,1,0:T(2,128)(2,1)} %reshape.205), channel_id=1, replica_groups=mesh['gx'=8,'fam'=4] {'gx'}, dimensions={0} | all-to-all | bytes 8388608 | tf_op jit(solution)/shard_map/all_to_all | solution.py:90
  314.5 10.3 %reshape.206 = bf16[512,1,64,64]{3,2,1,0:T(8,128)(2,1)} reshape(bf16[8,2,131072]{2,1,0:T(2,128)(2,1)} %all_to_all.30) | data formatting | bytes 8388608
  324.8 12.0 %copy.26 = bf16[64,1,64,8,64]{2,3,4,0,1:T(8,128)(2,1)} copy(bf16[64,1,64,8,64]{2,0,4,3,1:T(8,128)(2,1)} %bitcast.84) | data formatting | bytes 8388608 | tf_op jit(solution)/shard_map/all_to_all | solution.py:90
  336.7 12.3 %reshape.186 = bf16[64,512,64]{1,2,0:T(8,128)(2,1)} reshape(bf16[64,1,8,64,64]{3,2,4,0,1:T(8,128)(2,1)} %bitcast.85) | data formatting | bytes 8388608 | tf_op jit(solution)/shard_map/reshape.6
  349.0 7.7 fusion.13
  356.8 1.4 multiply_convert_fusion.1
  358.2 5.3 fusion.14
  363.5 3.5 fusion.5
  367.0 12.9 %copy.16 = bf16[64,1,512,64]{3,0,1,2:T(8,128)(2,1)} copy(bf16[64,1,512,64]{2,3,0,1:T(8,128)(2,1)} %fusion.5) | data formatting | bytes 8388608 | tf_op jit(solution)/shard_map/convert_element_type | solution.py:98
  379.9 10.5 %reshape.207 = bf16[8,2,131072]{2,1,0:T(2,128)(2,1)} reshape(bf16[512,1,64,64]{3,2,1,0:T(8,128)(2,1)} %bitcast.83) | data formatting | bytes 8388608
  390.4 4.5 all-to-all-start.1
  394.9 94.0 %all-to-all-done.1 = bf16[8,2,131072]{2,1,0:T(2,128)(2,1)} async-done(((bf16[8,2,131072]{2,1,0:T(2,128)(2,1)}), bf16[8,2,131072]{2,1,0:T(2,128)(2,1)}, u32[]{:S(2)}, u32[]{:S(2)}) %all-to-all-start.1) | async-done | bytes 4194336 | tf_op jit(solution)/shard_map/all_to_all | solution.py:99
  488.9 10.3 %reshape.208 = bf16[512,1,64,64]{3,2,1,0:T(8,128)(2,1)} reshape(bf16[8,2,131072]{2,1,0:T(2,128)(2,1)} %all-to-all-done.1) | data formatting | bytes 8388608
  499.2 12.0 %copy.25 = bf16[64,1,8,64,64]{4,2,3,0,1:T(8,128)(2,1)} copy(bf16[64,1,8,64,64]{4,0,3,2,1:T(8,128)(2,1)} %bitcast.86) | data formatting | bytes 8388608 | tf_op jit(solution)/shard_map/all_to_all | solution.py:99
  511.2 12.2 %reshape.188 = bf16[64,64,512]{2,1,0:T(8,128)(2,1)} reshape(bf16[64,1,64,8,64]{4,3,2,0,1:T(8,128)(2,1)} %bitcast.87) | data formatting | bytes 8388608 | tf_op jit(solution)/shard_map/reshape.11
  523.4 7.7 fusion.10
  531.1 0.0 copy-start.2
  531.1 2.0 fusion.3
  533.2 2.4 copy-done.2
  535.5 8.1 copy.18
  543.6 4.4 iota.35
  548.0 162.5 %sort.15 = (f32[64,1,64,512]{3,0,2,1:T(8,128)}, s32[64,1,64,512]{3,0,2,1:T(8,128)}) sort(f32[64,1,64,512]{3,0,2,1:T(8,128)} %copy.18, s32[64,1,64,512]{3,0,2,1:T(8,128)} %iota.35), dimensions={0}, to_apply=%region_0.1 | sort | flops 44040192 | bytes 33554432 | tf_op jit(solution)/shard_map/jit(sort)/sort | solution.py:104
  710.5 1.8 fusion.31
  712.4 10.1 %all_gather.6 = f32[4,1,64,512]{3,2,1,0:T(8,128)S(1)} all-gather(f32[1,1,64,512]{3,2,1,0:T(8,128)S(1)} %copy.19), channel_id=1, replica_groups=mesh['gx'=8,'fam'=4] {'fam'}, dimensions={0}, use_global_device_ids=true | all-gather | bytes 655360 | tf_op jit(solution)/shard_map/all_gather | solution.py:19
  722.5 10.2 %all_gather.7 = f32[4,1,64,512]{3,2,1,0:T(8,128)S(1)} all-gather(f32[1,1,64,512]{3,2,1,0:T(8,128)S(1)} %copy.20), channel_id=1, replica_groups=mesh['gx'=8,'fam'=4] {'fam'}, dimensions={0}, use_global_device_ids=true | all-gather | bytes 655360 | tf_op jit(solution)/shard_map/all_gather | solution.py:19
  732.8 0.3 while.15
  732.8 0.1 fusion.36
  732.9 0.1 fusion.36
  733.0 0.1 fusion.36
  733.1 4.8 multiply_bitcast_fusion
  737.9 0.2 fusion.30
  738.1 0.1 collective-permute-start
  738.2 3.5 collective-permute-start.1
  741.7 12.4 %collective-permute-done = f32[64,1,3,512]{3,2,0,1:T(4,128)S(1)} collective-permute-done((f32[64,1,3,512]{3,2,0,1:T(4,128)S(1)}, f32[64,1,3,512]{3,2,0,1:T(4,128)S(1)}, u32[]{:S(2)}, u32[]{:S(2)}) %collective-permute-start) | collective-permute-done | bytes 393248 | tf_op jit(solution)/shard_map/ppermute | solution.py:33
  754.2 0.0 collective-permute-done.1
  754.2 4.8 rsqrt_multiply_fusion
  759.0 3.1 fusion.28
  762.0 8.6 %fusion.29 = (f32[64,1,68,511]{3,2,0,1:T(8,128)}, f32[64,1,68,511]{3,2,0,1:T(8,128)}) fusion(f32[64,1,70,512]{3,2,0,1:T(8,128)S(1)} %get-tuple-element.64), kind=kLoop, calls=%fused_computation.65 | loop fusion | bytes 35581952 | tf_op jit(solution)/shard_map/jit(_roll_static)/slice | solution.py:56
  770.6 20.1 %multiply_subtract_fusion.1 = f32[64,1,68,512]{3,2,0,1:T(8,128)S(1)} fusion(f32[64,1,68,1]{3,2,0,1:T(8,128)} %get-tuple-element.66, f32[64,1,68,511]{3,2,0,1:T(8,128)} %get-tuple-element.68, f32[64,1,68,511]{3,2,0,1:T(8,128)} %get-tuple-element.67, f32[64,1,68,1]{3,2,0,1:T(8,128)} %get-tuple-element.65, f32[64,1,70,512]{3,2,0,1:T(8,128)S(1)} %get-tuple-element.64, ...), kind=kLoop, calls=%fused_computation.18 | loop fusion | flops 93585408 | bytes 62390272 | tf_op jit(solution)/shard_map/sub | solution.py:65
  790.7 3.1 fusion.26
  793.8 8.6 %fusion.27 = (f32[64,1,66,511]{3,2,0,1:T(8,128)}, f32[64,1,66,511]{3,2,0,1:T(8,128)}) fusion(f32[64,1,68,512]{3,2,0,1:T(8,128)S(1)} %multiply_subtract_fusion.1), kind=kLoop, calls=%fused_computation.63 | loop fusion | bytes 34535424 | tf_op jit(solution)/shard_map/jit(_roll_static)/slice | solution.py:56
  802.3 20.3 %multiply_subtract_fusion = f32[64,1,66,512]{3,2,0,1:T(8,128)S(1)} fusion(f32[64,1,66,1]{3,2,0,1:T(8,128)} %get-tuple-element.60, f32[64,1,66,511]{3,2,0,1:T(8,128)} %get-tuple-element.62, f32[64,1,66,511]{3,2,0,1:T(8,128)} %get-tuple-element.61, f32[64,1,66,1]{3,2,0,1:T(8,128)} %get-tuple-element.59, f32[64,1,68,512]{3,2,0,1:T(8,128)S(1)} %multiply_subtract_fusion.1, ...), kind=kLoop, calls=%fused_computation.17 | loop fusion | flops 90832896 | bytes 60555264 | tf_op jit(solution)/shard_map/sub | solution.py:65
  822.6 0.0 slice-start
  822.6 2.8 fusion.24
  825.4 0.0 slice-start.1
  825.4 0.0 slice-start.2
  825.4 7.7 fusion.25
  833.1 0.0 slice-done
  833.1 0.0 slice-done.1
  833.1 0.0 slice-done.2
  833.2 0.0 copy-start.1
  833.2 19.5 %subtract_bitcast_fusion = f32[64,1,64,512]{3,2,1,0:T(8,128)} fusion(f32[64,1,64,1]{3,2,0,1:T(8,128)} %get-tuple-element.56, f32[64,1,64,511]{3,2,0,1:T(8,128)} %get-tuple-element.58, f32[64,1,64,511]{3,2,0,1:T(8,128)} %get-tuple-element.57, f32[64,1,64,1]{3,2,0,1:T(8,128)} %get-tuple-element.55, f32[64,1,66,512]{3,2,0,1:T(8,128)S(1)} %multiply_subtract_fusion, ...), kind=kLoop, calls=%fused_computation.26 | loop fusion | flops 88080384 | bytes 58720256 | tf_op jit(solution)/shard_map/sub | solution.py:65
  852.7 0.0 copy-done.1
  (14 shorter events, 0.2 us)
Async XLA Ops:
  0.0 1.0 copy-start
  1.0 180.6 %copy-start.3 = (s32[1,64,512]{2,1,0:T(8,128)S(1)}, s32[1,64,512]{2,1,0:T(8,128)}, u32[]{:S(2)}) copy-start(s32[1,64,512]{2,1,0:T(8,128)} %param.4) | copy-start | bytes 393220
  390.4 98.6 %all-to-all-start.1 = ((bf16[8,2,131072]{2,1,0:T(2,128)(2,1)}), bf16[8,2,131072]{2,1,0:T(2,128)(2,1)}, u32[]{:S(2)}, u32[]{:S(2)}) async-start(bf16[8,2,131072]{2,1,0:T(2,128)(2,1)} %reshape.207), calls=%async_computation.1 | async-start | bytes 8388608 | tf_op jit(solution)/shard_map/all_to_all | solution.py:99
  531.1 4.4 copy-start.2
  738.1 16.0 %collective-permute-start = (f32[64,1,3,512]{3,2,0,1:T(4,128)S(1)}, f32[64,1,3,512]{3,2,0,1:T(4,128)S(1)}, u32[]{:S(2)}, u32[]{:S(2)}) collective-permute-start(f32[64,1,3,512]{3,2,0,1:T(4,128)S(1)} %get-tuple-element.69), channel_id=1, source_target_pairs={{0,4},{4,8},{8,12},{12,16},{16,20},{20,24},{24,28},{28,0},{1,5},{5... | collective-permute-start | bytes 1179656 | tf_op jit(solution)/shard_map/ppermute | solution.py:33
  738.2 16.0 %collective-permute-start.1 = (f32[64,1,3,512]{3,2,0,1:T(4,128)S(1)}, f32[64,1,3,512]{3,2,0,1:T(4,128)S(1)}, u32[]{:S(2)}, u32[]{:S(2)}) collective-permute-start(f32[64,1,3,512]{3,2,0,1:T(4,128)S(1)} %get-tuple-element.70), channel_id=1, source_target_pairs={{4,0},{8,4},{12,8},{16,12},{20,16},{24,20},{28,24},{0,28},{5,1},{9... | collective-permute-start | bytes 1179656 | tf_op jit(solution)/shard_map/ppermute | solution.py:34
  822.6 10.5 %slice-start = ((s8[9437184]{0:T(1024)(128)(4,1)}), s8[4194304]{0:T(1024)(128)(4,1)S(1)}, s32[]{:S(2)}) async-start(s8[9437184]{0:T(1024)(128)(4,1)} %bitcast.78), calls=%async_computation.2 | async-start | bytes 8388608
  825.4 7.7 slice-start.1
  825.4 7.7 slice-start.2
  833.2 19.5 %copy-start.1 = (s32[2048]{0:T(1024)S(1)}, s32[2048]{0:T(1024)}, u32[]{:S(2)}) copy-start(s32[2048]{0:T(1024)} %param.5) | copy-start | bytes 24580
where the time goes:
time: 860 us; the launch traced here: 853 us
  local copies, waits for them, and re-layouts  347 us (40%)
  other arithmetic  240 us (28%)
  blocking collectives  121 us (14%)
  waiting for transfers between devices  106 us (12%)
  matrix products  29.4 us (3%)
    gather x2, local copies, waits for them, and re-layouts, body(): owner = jnp.take(family_of_grain, labels, axis=0)  181 us
    sort x1, other arithmetic, body(): ordered = jnp.sort(u, axis=0)  162 us
    all_to_all x1, blocking collectives, body(): lax.all_to_all(spec_y, 'gx', split_axis=3, concat_axis=2, tiled=True)  101 us
    all_to_all x1, waiting for transfers between devices, body(): lax.all_to_all(lines_done, 'gx', split_axis=2, concat_axis=3, tiled=True)  94 us
    sub x3, other arithmetic, godunov(): return centre - step_size * sign * (grad - 1.0)  59.9 us
    unnamed x19, local copies, waits for them, and re-layouts  44 us
    slice x6, local copies, waits for them, and re-layouts, godunov(): jnp.roll(centre, 1, 3)  33.8 us
    another operation x3, local copies, waits for them, and re-layouts  28.9 us
  transfers between devices with their start and end apart: 3, of which 2 were waited for; matrix products, arithmetic and copies ran while one was open for 0% of the time, Pallas kernels for 0%

commit v1 on v0

v1 whole, which is shorter than its diff:
```python
import functools

import jax
import jax.numpy as jnp
import ml_dtypes
import numpy as np
from jax import lax
from jax.experimental import pallas as pl
from jax.experimental.pallas import tpu as pltpu
from jax.sharding import PartitionSpec as P

F = 256
WIDTH = 2
SWEEPS = 3
HALO = 8
LANES = 128
BIG = -1e30
MESH = pl.DeviceIdType.MESH

fidelity = 0.25
scale_factor = 8.0
step_size = 0.5


def smoothing(count):
    idx = np.arange(count).astype(np.float32)
    angle = (np.float32(2.0 * np.pi) * np.outer(idx, idx)) / np.float32(count)
    cas = (np.cos(angle) + np.sin(angle)).astype(ml_dtypes.bfloat16).astype(np.float64)
    freq = np.arange(count)
    mirror = np.minimum(freq, count - freq).astype(np.float64)
    sigma = WIDTH / 2.0
    gauss = np.exp(-2.0 * np.pi**2 * sigma**2 * mirror**2 / (count * count))
    full = (cas * gauss) @ cas.T / count
    high = full.astype(ml_dtypes.bfloat16)
    low = (full - high.astype(np.float64)).astype(ml_dtypes.bfloat16)
    return high, low


def ring_rows(x_local, count, parts):
    rows = x_local + HALO
    out = []
    for part in range(parts):
        r = np.arange(rows)
        x = part * x_local + np.where(r < x_local + HALO // 2, r, r - rows)
        out.append(x % count)
    return np.stack(out)


def owner_kernel(labels_ref, table_ref, out_ref):
    rows, cols = labels_ref.shape
    n_table = table_ref.shape[0]
    for c in range(cols // LANES):
        lab = labels_ref[:, c * LANES : (c + 1) * LANES]
        page = lab // LANES
        lane = lab % LANES
        acc = jnp.zeros((rows, LANES), jnp.int32)
        for k in range(n_table):
            row = jnp.broadcast_to(table_ref[k : k + 1, :], (rows, LANES))
            got = jnp.take_along_axis(row, lane, axis=1)
            acc = jnp.where(page == k, got, acc)
        out_ref[:, c * LANES : (c + 1) * LANES] = acc.astype(jnp.float32).astype(out_ref.dtype)


def owners(labels, table):
    return pl.pallas_call(
        owner_kernel,
        out_shape=jax.ShapeDtypeStruct(labels.shape, jnp.bfloat16),
        name="owner_lookup",
    )(labels, table)


def gather_kernel(axis, size, x_ref, out_ref, send_sem, recv_sem, local_sem):
    me = lax.axis_index(axis)
    barrier = pltpu.get_barrier_semaphore()
    for k in range(1, size):
        pl.semaphore_signal(
            barrier, inc=1, device_id={axis: lax.rem(me + k, size)}, device_id_type=MESH
        )
    local = pltpu.make_async_copy(x_ref, out_ref.at[me], local_sem)
    local.start()
    pl.semaphore_wait(barrier, size - 1)
    copies = []
    for k in range(1, size):
        copy = pltpu.make_async_remote_copy(
            src_ref=x_ref,
            dst_ref=out_ref.at[me],
            send_sem=send_sem.at[k - 1],
            recv_sem=recv_sem.at[k - 1],
            device_id={axis: lax.rem(me + k, size)},
            device_id_type=MESH,
        )
        copy.start()
        copies.append(copy)
    local.wait()
    for copy in copies:
        copy.wait()


def gathered(x, axis, size, collective_id):
    return pl.pallas_call(
        functools.partial(gather_kernel, axis, size),
        out_shape=jax.ShapeDtypeStruct((size, *x.shape), x.dtype),
        in_specs=[pl.BlockSpec(memory_space=pltpu.VMEM)],
        out_specs=pl.BlockSpec(memory_space=pltpu.VMEM),
        scratch_shapes=[
            pltpu.SemaphoreType.DMA((size - 1,)),
            pltpu.SemaphoreType.DMA((size - 1,)),
            pltpu.SemaphoreType.DMA,
        ],
        compiler_params=pltpu.CompilerParams(collective_id=collective_id, has_side_effects=True),
        name="gather_" + axis,
    )(x)


def smooth_kernel(
    x_local, fam_local, group,
    owner_ref, mx_ref, my_ref, u_ref, tops_ref, rel_ref, own_ref, t_ref,
):
    step = pl.program_id(0)
    nx, ny = owner_ref.shape
    rows = x_local + HALO
    x0 = lax.axis_index("gx") * x_local
    first = lax.axis_index("fam") * fam_local + step * group

    @pl.when(step == 0)
    def _():
        own_ref[0:x_local, :] = owner_ref[
            pl.ds(pl.multiple_of(x0, x_local), x_local), :
        ].astype(jnp.float32)
        after = lax.rem(x0 + x_local, nx)
        before = lax.rem(x0 + nx - 16, nx)
        right = owner_ref[pl.ds(pl.multiple_of(after, 16), 16), :].astype(jnp.float32)[0:HALO]
        left = owner_ref[pl.ds(pl.multiple_of(before, 16), 16), :].astype(jnp.float32)[HALO:16]
        place = lax.broadcasted_iota(jnp.int32, (HALO, ny), 0)
        own_ref[x_local:rows, :] = jnp.where(place < HALO // 2, right, left)
        tops_ref[...] = jnp.full(tops_ref.shape, BIG, jnp.float32)

    shift = jnp.full((nx, ny), first.astype(jnp.float32), jnp.float32).astype(jnp.bfloat16)
    rel_ref[...] = owner_ref[...] - shift
    mx = mx_ref[...]
    for j in range(group):
        chi = jnp.where(
            rel_ref[...] == jnp.bfloat16(j), jnp.bfloat16(1), jnp.bfloat16(0)
        )
        both = jnp.dot(mx, chi, preferred_element_type=jnp.float32)
        t_ref[j * rows : (j + 1) * rows, :] = both[:rows] + both[rows:]
    t = t_ref[...].astype(jnp.bfloat16)
    s = jnp.dot(t, my_ref[0], preferred_element_type=jnp.float32)
    for part in range(1, my_ref.shape[0]):
        s = s + jnp.dot(t, my_ref[part], preferred_element_type=jnp.float32)
    t_ref[...] = s
    base = first.astype(jnp.float32)
    for r in range(rows // 8):
        strip = slice(8 * r, 8 * r + 8)
        own = own_ref[strip, :] - base
        high, second = tops_ref[0, strip, :], tops_ref[1, strip, :]
        for j in range(group):
            u = t_ref[j * rows + 8 * r : j * rows + 8 * r + 8, :]
            u = u + jnp.where(own == float(j), fidelity, 0.0)
            u_ref[j, strip, :] = u
            second = jnp.maximum(second, jnp.minimum(high, u))
            high = jnp.maximum(high, u)
        tops_ref[0, strip, :] = high
        tops_ref[1, strip, :] = second


def smoothed(owner, mx, my, x_local, fam_local):
    nx, ny = owner.shape
    rows = x_local + HALO
    group = min(8, fam_local)
    return pl.pallas_call(
        functools.partial(smooth_kernel, x_local, fam_local, group),
        grid=(fam_local // group,),
        out_shape=(
            jax.ShapeDtypeStruct((fam_local, rows, ny), jnp.float32),
            jax.ShapeDtypeStruct((2, rows, ny), jnp.float32),
        ),
        in_specs=[
            pl.BlockSpec((nx, ny), lambda i: (0, 0)),
            pl.BlockSpec(mx.shape, lambda i: (0, 0)),
            pl.BlockSpec(my.shape, lambda i: (0, 0, 0)),
        ],
        out_specs=(
            pl.BlockSpec((group, rows, ny), lambda i: (i, 0, 0)),
            pl.BlockSpec((2, rows, ny), lambda i: (0, 0, 0)),
        ),
        scratch_shapes=[
            pltpu.VMEM((nx, ny), jnp.bfloat16),
            pltpu.VMEM((rows, ny), jnp.float32),
            pltpu.VMEM((group * rows, ny), jnp.float32),
        ],
        compiler_params=pltpu.CompilerParams(vmem_limit_bytes=40 * 2**20),
        name="smooth",
    )(owner, mx, my)


def redistance_kernel(x_local, group, tops_ref, u_ref, out_ref, top_ref, phi_ref, sig_ref, half_ref):
    rows, ny = u_ref.shape[1:]
    chunks = ny // LANES
    strips = rows // 8

    @pl.when(pl.program_id(0) == 0)
    def _():
        for r in range(strips):
            strip = slice(8 * r, 8 * r + 8)
            high, second = tops_ref[0, 0, strip, :], tops_ref[0, 1, strip, :]
            for part in range(1, tops_ref.shape[0]):
                other, third = tops_ref[part, 0, strip, :], tops_ref[part, 1, strip, :]
                second = jnp.maximum(jnp.minimum(high, other), jnp.maximum(second, third))
                high = jnp.maximum(high, other)
            top_ref[0, strip, :] = high
            top_ref[1, strip, :] = second

    lane = lax.broadcasted_iota(jnp.int32, (8, LANES), 1)
    is_first, is_last = lane == 0, lane == LANES - 1

    def put(slot, r, c, value):
        phi_ref[slot, c, 8 * r + HALO : 8 * r + HALO + 8, :] = value
        if r == strips - 1:
            phi_ref[slot, c, 0:HALO, :] = value

    def one(j, carry):
        for r in range(strips):
            for c in range(chunks):
                rs, cs = slice(8 * r, 8 * r + 8), slice(c * LANES, (c + 1) * LANES)
                u = u_ref[j, rs, cs]
                top1 = top_ref[0, rs, cs]
                phi = scale_factor * (u - jnp.where(u >= top1, top_ref[1, rs, cs], top1))
                put(0, r, c, phi)
                sig_ref[c, rs, :] = jnp.where(phi > 0.0, 1.0, -1.0)
                half_ref[c, rs, :] = phi * (step_size * lax.rsqrt(phi * phi + 1.0))
        for sweep in range(SWEEPS):
            src, dst = sweep % 2, (sweep + 1) % 2
            final = sweep == SWEEPS - 1
            for r in range(x_local // 8 if final else strips):
                rs = slice(8 * r, 8 * r + 8)
                mid = [phi_ref[src, c, 8 * r + HALO : 8 * r + HALO + 8, :] for c in range(chunks)]
                to_right = [pltpu.roll(v, 1, 1) for v in mid]
                to_left = [pltpu.roll(v, LANES - 1, 1) for v in mid]
                for c in range(chunks):
                    sig, half, centre = sig_ref[c, rs, :], half_ref[c, rs, :], mid[c]
                    y_low = jnp.where(is_first, to_right[c - 1], to_right[c])
                    y_high = jnp.where(is_last, to_left[(c + 1) % chunks], to_left[c])
                    x_low = phi_ref[src, c, 8 * r + HALO - 1 : 8 * r + HALO + 7, :]
                    if r == strips - 1:
                        x_high = phi_ref[src, c, 1:9, :]
                    else:
                        x_high = phi_ref[src, c, 8 * r + HALO + 1 : 8 * r + HALO + 9, :]
                    here = centre * sig
                    gx = jnp.maximum(here - jnp.minimum(x_low * sig, x_high * sig), 1e-18)
                    gy = jnp.maximum(here - jnp.minimum(y_low * sig, y_high * sig), 1e-18)
                    square = gx * gx + gy * gy
                    grad = square * lax.rsqrt(square)
                    new = centre - half * (grad - 1.0)
                    if final:
                        out_ref[j, rs, c * LANES : (c + 1) * LANES] = new
                    else:
                        put(dst, r, c, new)
        return carry

    lax.fori_loop(0, group, one, 0)


def redistanced(tops, u, x_local):
    fam_local, rows, ny = u.shape
    group = min(8, fam_local)
    chunks = ny // LANES
    return pl.pallas_call(
        functools.partial(redistance_kernel, x_local, group),
        grid=(fam_local // group,),
        out_shape=jax.ShapeDtypeStruct((fam_local, x_local, ny), jnp.float32),
        in_specs=[
            pl.BlockSpec(tops.shape, lambda i: (0, 0, 0, 0)),
            pl.BlockSpec((group, rows, ny), lambda i: (i, 0, 0)),
        ],
        out_specs=pl.BlockSpec((group, x_local, ny), lambda i: (i, 0, 0)),
        scratch_shapes=[
            pltpu.VMEM((2, rows, ny), jnp.float32),
            pltpu.VMEM((2, chunks, rows + HALO, LANES), jnp.float32),
            pltpu.VMEM((chunks, rows, LANES), jnp.float32),
            pltpu.VMEM((chunks, rows, LANES), jnp.float32),
        ],
        compiler_params=pltpu.CompilerParams(vmem_limit_bytes=40 * 2**20),
        name="redistance",
    )(tops, u)


def body(labels, family_of_grain, mx, my):
    parts, fams = lax.axis_size("gx"), lax.axis_size("fam")
    nz, x_local, ny = labels.shape
    assert nz == 1
    nx = x_local * parts
    fam_local = F // fams
    owner = owners(labels[0], family_of_grain.reshape(-1, LANES))
    owner = gathered(owner, "gx", parts, 0).reshape(nx, ny)
    u, tops = smoothed(owner, mx[0], my, x_local, fam_local)
    tops = gathered(tops, "fam", fams, 1)
    return redistanced(tops, u, x_local)[:, None]


def solution(mesh):
    def run(labels, family_of_grain):
        nz, nx, ny = labels.shape
        parts = mesh.shape["gx"]
        high, low = smoothing(nx)
        rows = ring_rows(nx // parts, nx, parts)
        mx = jnp.asarray(np.concatenate([high[rows], low[rows]], axis=1))
        my = jnp.asarray(smoothing(ny)[0][None])
        mapped = jax.shard_map(
            body,
            mesh=mesh,
            in_specs=(P(None, "gx", None), P(), P("gx", None, None), P()),
            out_specs=P("fam", None, "gx", None),
            check_vma=False,
        )
        return mapped(labels, family_of_grain, mx, my)

    return run
```

time: 860 us -> 87.3 us (0.10)
  local copies, waits for them, and re-layouts: 347 us -> 12.5 us
  other arithmetic: 240 us -> 0 us
  blocking collectives: 121 us -> 0 us
  waiting for transfers between devices: 106 us -> 0 us
  Pallas kernels: 0 us -> 73.2 us
  matrix products: 29.4 us -> 0 us
    gather x2 -> x0, local copies, waits for them, and re-layouts: 181 us -> none  [body(): owner = jnp.take(family_of_grain, labels, axis=0)]
    sort x1 -> x0, other arithmetic: 162 us -> none  [body(): ordered = jnp.sort(u, axis=0)]
    all_to_all x1 -> x0, blocking collectives: 101 us -> none  [body(): lax.all_to_all(spec_y, 'gx', split_axis=3, concat_axis=2, tiled=True)]
    all_to_all x1 -> x0, waiting for transfers between devices: 94 us -> none  [body(): lax.all_to_all(lines_done, 'gx', split_axis=2, concat_axis=3, tiled=True)]
    pallas_call x0 -> x5, Pallas kernels: none -> 73.2 us  [the longest x2 34.9 us: gathered(): pl.pallas_call(functools.partial(gather_kernel, axis, size), out_shape=ja...]
    sub x3 -> x0, other arithmetic: 59.9 us -> none  [godunov(): return centre - step_size * sign * (grad - 1.0)]
    slice x12 -> x0, local copies, waits for them, and re-layouts: 35.9 us -> none  [the longest x6 33.8 us: godunov(): jnp.roll(centre, 1, 3)]
    unnamed x19 -> x13, local copies, waits for them, and re-layouts: 44 us -> 11.6 us
  transfers between devices with their start and end apart: 3 -> 0, of which waited for: 2 -> 0; matrix products, arithmetic and copies ran while one was open for 0% -> 0% of each run, Pallas kernels for 0% -> 0%
where the time goes in v1:
time: 87.3 us; the launch traced here: 86.5 us
  Pallas kernels  73.2 us (84%)
  local copies, waits for them, and re-layouts  12.5 us (14%)
    pallas_call x2, Pallas kernels, gathered(): pl.pallas_call(functools.partial(gather_kernel, axis, size), out_shape=ja...  34.9 us
    pallas_call x1, Pallas kernels, redistanced(): pl.pallas_call(functools.partial(redistance_kernel, x_local, group), grid...  25.6 us
    unnamed x13, local copies, waits for them, and re-layouts  11.6 us
    pallas_call x1, Pallas kernels, smoothed(): pl.pallas_call(functools.partial(smooth_kernel, x_local, fam_local, group...  9.62 us
    pallas_call x1, Pallas kernels, owners(): pl.pallas_call(owner_kernel, out_shape=jax.ShapeDtypeStruct(labels.shape,...  3.05 us

profile of v1, /device:TPU:0, one launch (start us, length us, event | category | flops | bytes accessed | tf_op | source)
XLA Modules:
  0.0 86.5 jit_solution(17191619171719371343)
XLA Ops:
  0.0 0.0 copy-start.4
  0.0 1.3 %dynamic-slice = u32[1]{0:T(128)} dynamic-slice(u32[32]{0:T(128)} %constant.7, u32[]{:T(128)S(6)} %partition-id.1), dynamic_slice_sizes={1} | dynamic-slice | bytes 12
  1.9 3.1 %owner_lookup.1.x_ref = bf16[64,512]{1,0:T(8,128)(2,1)} custom-call(s32[64,512]{1,0:T(8,128)} %bitcast.10, s32[16,128]{1,0:T(8,128)} %bitcast.11), custom_call_target="tpu_custom_call" | custom-call | tf_op jit(solution)/shard_map/owner_lookup/pallas_call | solution.py:65
  5.0 0.9 %dynamic-slice_bitcast_fusion.mx_ref = bf16[144,512]{1,0:T(8,128)(2,1)S(1)} fusion(bf16[8,144,512]{2,1,0:T(8,128)(2,1)} %constant.6, s32[]{:T(128)} %bitcast.3), kind=kLoop, calls=%fused_computation | loop fusion | bytes 294916 | tf_op jit(solution)/shard_map/squeeze | solution.py:296
  5.9 15.8 %gather_gx.1 = bf16[8,64,512]{2,1,0:T(8,128)(2,1)} custom-call(bf16[64,512]{1,0:T(8,128)(2,1)} %owner_lookup.1.x_ref), custom_call_target="tpu_custom_call" | custom-call | tf_op jit(solution)/shard_map/gather_gx/pallas_call | solution.py:100
  21.8 0.0 copy-done.4
  21.8 0.0 copy-start.3
  21.8 1.0 %copy-done.3 = bf16[8,64,512]{2,1,0:T(8,128)(2,1)S(1)} copy-done((bf16[8,64,512]{2,1,0:T(8,128)(2,1)S(1)}, bf16[8,64,512]{2,1,0:T(8,128)(2,1)}, u32[]{:S(2)}) %copy-start.3) | copy-done | bytes 524312
  22.8 9.6 %smooth.1 = (f32[64,72,512]{2,1,0:T(8,128)S(1)}, f32[2,72,512]{2,1,0:T(8,128)S(1)}) custom-call(bf16[512,512]{1,0:T(8,128)(2,1)S(1)} %bitcast.9, bf16[144,512]{1,0:T(8,128)(2,1)S(1)} %dynamic-slice_bitcast_fusion.mx_ref, bf16[1,512,512]{2,1,0:T(8,128)(2,1)S(1)} %copy-done.4), custom_call_target="tpu_custom_call" | custom-call | tf_op jit(solution)/shard_map/smooth/pallas_call | solution.py:171
  32.5 0.0 copy-start
  32.5 3.6 %copy-done = f32[64,72,512]{2,1,0:T(8,128)} copy-done((f32[64,72,512]{2,1,0:T(8,128)}, f32[64,72,512]{2,1,0:T(8,128)S(1)}, u32[]{:S(2)}) %copy-start) | copy-done | bytes 9437208
  36.1 0.0 copy-start.5
  36.1 0.7 copy-done.5
  36.8 19.1 %gather_fam.1.tops_ref = f32[4,2,72,512]{3,2,1,0:T(8,128)} custom-call(f32[2,72,512]{2,1,0:T(8,128)} %copy-done.5), custom_call_target="tpu_custom_call" | custom-call | tf_op jit(solution)/shard_map/gather_fam/pallas_call | solution.py:100
  55.9 0.0 copy-start.1
  55.9 3.7 %copy-done.1 = f32[64,72,512]{2,1,0:T(8,128)S(1)} copy-done((f32[64,72,512]{2,1,0:T(8,128)S(1)}, f32[64,72,512]{2,1,0:T(8,128)}, u32[]{:S(2)}) %copy-start.1) | copy-done | bytes 9437208
  59.6 0.0 copy-start.2
  59.6 1.3 %copy-done.2 = f32[4,2,72,512]{3,2,1,0:T(8,128)S(1)} copy-done((f32[4,2,72,512]{3,2,1,0:T(8,128)S(1)}, f32[4,2,72,512]{3,2,1,0:T(8,128)}, u32[]{:S(2)}) %copy-start.2) | copy-done | bytes 1179672
  60.8 25.6 %redistance.1 = f32[64,64,512]{2,1,0:T(8,128)} custom-call(f32[4,2,72,512]{3,2,1,0:T(8,128)S(1)} %copy-done.2, f32[64,72,512]{2,1,0:T(8,128)S(1)} %copy-done.1), custom_call_target="tpu_custom_call" | custom-call | tf_op jit(solution)/shard_map/redistance/pallas_call | solution.py:268
Async XLA Ops:
  0.0 21.8 %copy-start.4 = (bf16[1,512,512]{2,1,0:T(8,128)(2,1)S(1)}, bf16[1,512,512]{2,1,0:T(8,128)(2,1)}, u32[]{:S(2)}) copy-start(bf16[1,512,512]{2,1,0:T(8,128)(2,1)} %constant.5.clone.my_ref) | copy-start | bytes 1572868
  21.8 1.0 %copy-start.3 = (bf16[8,64,512]{2,1,0:T(8,128)(2,1)S(1)}, bf16[8,64,512]{2,1,0:T(8,128)(2,1)}, u32[]{:S(2)}) copy-start(bf16[8,64,512]{2,1,0:T(8,128)(2,1)} %gather_gx.1) | copy-start | bytes 1572868
  32.5 3.6 %copy-start = (f32[64,72,512]{2,1,0:T(8,128)}, f32[64,72,512]{2,1,0:T(8,128)S(1)}, u32[]{:S(2)}) copy-start(f32[64,72,512]{2,1,0:T(8,128)S(1)} %get-tuple-element.8.u_ref) | copy-start | bytes 28311556
  36.1 0.7 copy-start.5
  55.9 3.7 %copy-start.1 = (f32[64,72,512]{2,1,0:T(8,128)S(1)}, f32[64,72,512]{2,1,0:T(8,128)}, u32[]{:S(2)}) copy-start(f32[64,72,512]{2,1,0:T(8,128)} %copy-done) | copy-start | bytes 28311556
  59.6 1.3 %copy-start.2 = (f32[4,2,72,512]{3,2,1,0:T(8,128)S(1)}, f32[4,2,72,512]{3,2,1,0:T(8,128)}, u32[]{:S(2)}) copy-start(f32[4,2,72,512]{3,2,1,0:T(8,128)} %gather_fam.1.tops_ref) | copy-start | bytes 3538948

commit v2 on v1

--- a/solution.py
+++ b/solution.py
@@ -15,6 +15,7 @@
 HALO = 8
 LANES = 128
 BIG = -1e30
+VMEM = 60 * 2**20
 MESH = pl.DeviceIdType.MESH
 
 fidelity = 0.25
@@ -48,16 +49,21 @@
 
 def owner_kernel(labels_ref, table_ref, out_ref):
     rows, cols = labels_ref.shape
-    n_table = table_ref.shape[0]
+    words = []
+    for k in range(table_ref.shape[0] // 4):
+        quad = [table_ref[4 * k + b : 4 * k + b + 1, :] for b in range(4)]
+        word = quad[0] + quad[1] * 2**8 + quad[2] * 2**16 + lax.shift_left(quad[3], 24)
+        words.append(jnp.broadcast_to(word, (rows, LANES)))
     for c in range(cols // LANES):
         lab = labels_ref[:, c * LANES : (c + 1) * LANES]
-        page = lab // LANES
-        lane = lab % LANES
-        acc = jnp.zeros((rows, LANES), jnp.int32)
-        for k in range(n_table):
-            row = jnp.broadcast_to(table_ref[k : k + 1, :], (rows, LANES))
-            got = jnp.take_along_axis(row, lane, axis=1)
-            acc = jnp.where(page == k, got, acc)
+        lane = lax.bitwise_and(lab, LANES - 1)
+        page = lax.shift_right_logical(lab, LANES.bit_length() - 1)
+        which = lax.shift_right_logical(page, 2)
+        place = lax.bitwise_and(page, 3) * 8
+        acc = jnp.take_along_axis(words[0], lane, axis=1)
+        for k in range(1, len(words)):
+            acc = jnp.where(which == k, jnp.take_along_axis(words[k], lane, axis=1), acc)
+        acc = lax.bitwise_and(lax.shift_right_logical(acc, place), 255)
         out_ref[:, c * LANES : (c + 1) * LANES] = acc.astype(jnp.float32).astype(out_ref.dtype)
 
 
@@ -65,34 +71,46 @@
     return pl.pallas_call(
         owner_kernel,
         out_shape=jax.ShapeDtypeStruct(labels.shape, jnp.bfloat16),
+        compiler_params=pltpu.CompilerParams(vmem_limit_bytes=VMEM),
         name="owner_lookup",
     )(labels, table)
 
 
 def gather_kernel(axis, size, x_ref, out_ref, send_sem, recv_sem, local_sem):
     me = lax.axis_index(axis)
+    chips = size // 2
+    chip, core = me // 2, lax.rem(me, 2)
+    beside = 2 * chip + 1 - core
+    others = [2 * lax.rem(chip + d, chips) + core for d in range(1, chips)]
     barrier = pltpu.get_barrier_semaphore()
-    for k in range(1, size):
-        pl.semaphore_signal(
-            barrier, inc=1, device_id={axis: lax.rem(me + k, size)}, device_id_type=MESH
-        )
+    for device in [beside, *others]:
+        pl.semaphore_signal(barrier, inc=1, device_id={axis: device}, device_id_type=MESH)
     local = pltpu.make_async_copy(x_ref, out_ref.at[me], local_sem)
     local.start()
-    pl.semaphore_wait(barrier, size - 1)
-    copies = []
-    for k in range(1, size):
+    pl.semaphore_wait(barrier, chips)
+
+    def send(src, slab, device, k):
         copy = pltpu.make_async_remote_copy(
-            src_ref=x_ref,
-            dst_ref=out_ref.at[me],
-            send_sem=send_sem.at[k - 1],
-            recv_sem=recv_sem.at[k - 1],
-            device_id={axis: lax.rem(me + k, size)},
+            src_ref=src,
+            dst_ref=out_ref.at[slab],
+            send_sem=send_sem.at[k],
+            recv_sem=recv_sem.at[k],
+            device_id={axis: device},
             device_id_type=MESH,
         )
         copy.start()
-        copies.append(copy)
+        return copy
+
+    far = [send(x_ref, me, device, d) for d, device in enumerate(others)]
+    near = [send(x_ref, me, beside, chips - 1)]
+    for d in range(1, chips):
+        far[d - 1].wait_recv()
+        slab = 2 * lax.rem(chip + chips - d, chips) + core
+        near.append(send(out_ref.at[slab], slab, beside, chips - 1 + d))
     local.wait()
-    for copy in copies:
+    for copy in far:
+        copy.wait_send()
+    for copy in near:
         copy.wait()
 
 
@@ -107,9 +125,73 @@
             pltpu.SemaphoreType.DMA((size - 1,)),
             pltpu.SemaphoreType.DMA,
         ],
-        compiler_params=pltpu.CompilerParams(collective_id=collective_id, has_side_effects=True),
+        compiler_params=pltpu.CompilerParams(
+            collective_id=collective_id, has_side_effects=True, vmem_limit_bytes=VMEM
+        ),
         name="gather_" + axis,
     )(x)
+
+
+def merge_kernel(axis, size, x_ref, out_ref, recv_ref, send_sem, recv_sem, back_send, back_recv):
+    me = lax.axis_index(axis)
+    others = [lax.rem(me + k, size) for k in range(1, size)]
+    barrier = pltpu.get_barrier_semaphore()
+    for device in others:
+        pl.semaphore_signal(barrier, inc=1, device_id={axis: device}, device_id_type=MESH)
+    pl.semaphore_wait(barrier, size - 1)
+
+    def send(src, dst, sems, k, device):
+        copy = pltpu.make_async_remote_copy(
+            src_ref=src,
+            dst_ref=dst,
+            send_sem=sems[0].at[k],
+            recv_sem=sems[1].at[k],
+            device_id={axis: device},
+            device_id_type=MESH,
+        )
+        copy.start()
+        return copy
+
+    there = [
+        send(x_ref.at[device], recv_ref.at[k], (send_sem, recv_sem), k, device)
+        for k, device in enumerate(others)
+    ]
+    high, second = x_ref[me, 0], x_ref[me, 1]
+    for k in range(size - 1):
+        there[k].wait_recv()
+        other, third = recv_ref[k, 0], recv_ref[k, 1]
+        second = jnp.maximum(jnp.minimum(high, other), jnp.maximum(second, third))
+        high = jnp.maximum(high, other)
+    out_ref[me, 0] = high
+    out_ref[me, 1] = second
+    back = [
+        send(out_ref.at[me], out_ref.at[me], (back_send, back_recv), k, device)
+        for k, device in enumerate(others)
+    ]
+    for copy in there:
+        copy.wait_send()
+    for copy in back:
+        copy.wait()
+
+
+def merged(x, axis, size, collective_id):
+    return pl.pallas_call(
+        functools.partial(merge_kernel, axis, size),
+        out_shape=jax.ShapeDtypeStruct(x.shape, x.dtype),
+        in_specs=[pl.BlockSpec(memory_space=pltpu.VMEM)],
+        out_specs=pl.BlockSpec(memory_space=pltpu.VMEM),
+        scratch_shapes=[pltpu.VMEM((size - 1, *x.shape[1:]), x.dtype)]
+        + [pltpu.SemaphoreType.DMA((size - 1,))] * 4,
+        compiler_params=pltpu.CompilerParams(
+            collective_id=collective_id, has_side_effects=True, vmem_limit_bytes=VMEM
+        ),
+        name="merge_" + axis,
+    )(x)
+
+
+def tile_place(k, per_piece):
+    row = 8 * (k % per_piece)
+    return k // per_piece, slice(row, row + 8)
 
 
 def smooth_kernel(
@@ -137,7 +219,7 @@
 
     shift = jnp.full((nx, ny), first.astype(jnp.float32), jnp.float32).astype(jnp.bfloat16)
     rel_ref[...] = owner_ref[...] - shift
-    mx = mx_ref[...]
+    mx = mx_ref[0]
     for j in range(group):
         chi = jnp.where(
             rel_ref[...] == jnp.bfloat16(j), jnp.bfloat16(1), jnp.bfloat16(0)
@@ -150,67 +232,62 @@
         s = s + jnp.dot(t, my_ref[part], preferred_element_type=jnp.float32)
     t_ref[...] = s
     base = first.astype(jnp.float32)
+    per_piece = tops_ref.shape[2] // 8
     for r in range(rows // 8):
         strip = slice(8 * r, 8 * r + 8)
-        own = own_ref[strip, :] - base
-        high, second = tops_ref[0, strip, :], tops_ref[1, strip, :]
-        for j in range(group):
-            u = t_ref[j * rows + 8 * r : j * rows + 8 * r + 8, :]
-            u = u + jnp.where(own == float(j), fidelity, 0.0)
-            u_ref[j, strip, :] = u
-            second = jnp.maximum(second, jnp.minimum(high, u))
-            high = jnp.maximum(high, u)
-        tops_ref[0, strip, :] = high
-        tops_ref[1, strip, :] = second
-
-
-def smoothed(owner, mx, my, x_local, fam_local):
+        for c in range(ny // LANES):
+            cols = slice(c * LANES, (c + 1) * LANES)
+            piece, place = tile_place(r * (ny // LANES) + c, per_piece)
+            own = own_ref[strip, cols] - base
+            high, second = tops_ref[piece, 0, place, :], tops_ref[piece, 1, place, :]
+            for j in range(group):
+                u = t_ref[j * rows + 8 * r : j * rows + 8 * r + 8, cols]
+                u = u + jnp.where(own == float(j), fidelity, 0.0)
+                u_ref[j, strip, cols] = u
+                second = jnp.maximum(second, jnp.minimum(high, u))
+                high = jnp.maximum(high, u)
+            tops_ref[piece, 0, place, :] = high
+            tops_ref[piece, 1, place, :] = second
+
+
+def smoothed(owner, mx, my, x_local, fam_local, fams):
     nx, ny = owner.shape
     rows = x_local + HALO
     group = min(8, fam_local)
+    tiles = rows * ny // (8 * LANES)
+    pieces = (fams, 2, 8 * (-(-tiles // fams)), LANES)
     return pl.pallas_call(
         functools.partial(smooth_kernel, x_local, fam_local, group),
         grid=(fam_local // group,),
         out_shape=(
             jax.ShapeDtypeStruct((fam_local, rows, ny), jnp.float32),
-            jax.ShapeDtypeStruct((2, rows, ny), jnp.float32),
+            jax.ShapeDtypeStruct(pieces, jnp.float32),
         ),
         in_specs=[
             pl.BlockSpec((nx, ny), lambda i: (0, 0)),
-            pl.BlockSpec(mx.shape, lambda i: (0, 0)),
+            pl.BlockSpec((1, *mx.shape[1:]), lambda i: (lax.axis_index("gx"), 0, 0)),
             pl.BlockSpec(my.shape, lambda i: (0, 0, 0)),
         ],
         out_specs=(
             pl.BlockSpec((group, rows, ny), lambda i: (i, 0, 0)),
-            pl.BlockSpec((2, rows, ny), lambda i: (0, 0, 0)),
+            pl.BlockSpec(pieces, lambda i: (0, 0, 0, 0)),
         ),
         scratch_shapes=[
             pltpu.VMEM((nx, ny), jnp.bfloat16),
             pltpu.VMEM((rows, ny), jnp.float32),
             pltpu.VMEM((group * rows, ny), jnp.float32),
         ],
-        compiler_params=pltpu.CompilerParams(vmem_limit_bytes=40 * 2**20),
+        compiler_params=pltpu.CompilerParams(vmem_limit_bytes=VMEM),
         name="smooth",
     )(owner, mx, my)
 
 
-def redistance_kernel(x_local, group, tops_ref, u_ref, out_ref, top_ref, phi_ref, sig_ref, half_ref):
+def redistance_kernel(x_local, group, tops_ref, u_ref, out_ref, phi_ref, sig_ref, half_ref):
     rows, ny = u_ref.shape[1:]
     chunks = ny // LANES
     strips = rows // 8
 
-    @pl.when(pl.program_id(0) == 0)
-    def _():
-        for r in range(strips):
-            strip = slice(8 * r, 8 * r + 8)
-            high, second = tops_ref[0, 0, strip, :], tops_ref[0, 1, strip, :]
-            for part in range(1, tops_ref.shape[0]):
-                other, third = tops_ref[part, 0, strip, :], tops_ref[part, 1, strip, :]
-                second = jnp.maximum(jnp.minimum(high, other), jnp.maximum(second, third))
-                high = jnp.maximum(high, other)
-            top_ref[0, strip, :] = high
-            top_ref[1, strip, :] = second
-
+    per_piece = tops_ref.shape[2] // 8
     lane = lax.broadcasted_iota(jnp.int32, (8, LANES), 1)
     is_first, is_last = lane == 0, lane == LANES - 1
 
@@ -224,8 +301,9 @@
             for c in range(chunks):
                 rs, cs = slice(8 * r, 8 * r + 8), slice(c * LANES, (c + 1) * LANES)
                 u = u_ref[j, rs, cs]
-                top1 = top_ref[0, rs, cs]
-                phi = scale_factor * (u - jnp.where(u >= top1, top_ref[1, rs, cs], top1))
+                piece, place = tile_place(r * chunks + c, per_piece)
+                top1, top2 = tops_ref[piece, 0, place, :], tops_ref[piece, 1, place, :]
+                phi = scale_factor * (u - jnp.where(u >= top1, top2, top1))
                 put(0, r, c, phi)
                 sig_ref[c, rs, :] = jnp.where(phi > 0.0, 1.0, -1.0)
                 half_ref[c, rs, :] = phi * (step_size * lax.rsqrt(phi * phi + 1.0))
@@ -275,12 +353,11 @@
         ],
         out_specs=pl.BlockSpec((group, x_local, ny), lambda i: (i, 0, 0)),
         scratch_shapes=[
-            pltpu.VMEM((2, rows, ny), jnp.float32),
             pltpu.VMEM((2, chunks, rows + HALO, LANES), jnp.float32),
             pltpu.VMEM((chunks, rows, LANES), jnp.float32),
             pltpu.VMEM((chunks, rows, LANES), jnp.float32),
         ],
-        compiler_params=pltpu.CompilerParams(vmem_limit_bytes=40 * 2**20),
+        compiler_params=pltpu.CompilerParams(vmem_limit_bytes=VMEM),
         name="redistance",
     )(tops, u)
 
@@ -293,8 +370,8 @@
     fam_local = F // fams
     owner = owners(labels[0], family_of_grain.reshape(-1, LANES))
     owner = gathered(owner, "gx", parts, 0).reshape(nx, ny)
-    u, tops = smoothed(owner, mx[0], my, x_local, fam_local)
-    tops = gathered(tops, "fam", fams, 1)
+    u, tops = smoothed(owner, mx, my, x_local, fam_local, fams)
+    tops = merged(tops, "fam", fams, 1)
     return redistanced(tops, u, x_local)[:, None]
 
 
@@ -309,7 +386,7 @@
         mapped = jax.shard_map(
             body,
             mesh=mesh,
-            in_specs=(P(None, "gx", None), P(), P("gx", None, None), P()),
+            in_specs=(P(None, "gx", None), P(), P(), P()),
             out_specs=P("fam", None, "gx", None),
             check_vma=False,
         )

time: 87.3 us -> 69.3 us (0.79)
  local copies, waits for them, and re-layouts: 12.5 us -> 0 us
  Pallas kernels: 73.2 us -> 69 us
    pallas_call x2 -> x1, Pallas kernels: 34.9 us -> 13.5 us  [gathered(): pl.pallas_call(functools.partial(gather_kernel, axis, size), out_shape=ja...]
    pallas_call x0 -> x1, Pallas kernels: none -> 14.4 us  [merged(): pl.pallas_call(functools.partial(merge_kernel, axis, size), out_shape=jax...]
    unnamed x13 -> x0, local copies, waits for them, and re-layouts: 11.6 us -> none
    pallas_call x1, Pallas kernels: 9.62 us -> 12.2 us  [smoothed(): pl.pallas_call(functools.partial(smooth_kernel, x_local, fam_local, group...]
    pallas_call x1, Pallas kernels: 25.6 us -> 26.9 us  [redistanced(): pl.pallas_call(functools.partial(redistance_kernel, x_local, group), grid...]
    pallas_call x1, Pallas kernels: 3.05 us -> 1.97 us  [owners(): pl.pallas_call(owner_kernel, out_shape=jax.ShapeDtypeStruct(labels.shape,...]
    squeeze x1 -> x0, local copies, waits for them, and re-layouts: 0.92 us -> none  [body(): u, tops = smoothed(owner, mx[0], my, x_local, fam_local)]
where the time goes in v2:
time: 69.3 us; the launch traced here: 69 us
  Pallas kernels  69 us (100%)
    pallas_call x1, Pallas kernels, redistanced(): pl.pallas_call(functools.partial(redistance_kernel, x_local, group), grid...  26.9 us
    pallas_call x1, Pallas kernels, merged(): pl.pallas_call(functools.partial(merge_kernel, axis, size), out_shape=jax...  14.4 us
    pallas_call x1, Pallas kernels, gathered(): pl.pallas_call(functools.partial(gather_kernel, axis, size), out_shape=ja...  13.5 us
    pallas_call x1, Pallas kernels, smoothed(): pl.pallas_call(functools.partial(smooth_kernel, x_local, fam_local, group...  12.2 us
    pallas_call x1, Pallas kernels, owners(): pl.pallas_call(owner_kernel, out_shape=jax.ShapeDtypeStruct(labels.shape,...  1.97 us

profile of v2, /device:TPU:0, one launch (start us, length us, event | category | flops | bytes accessed | tf_op | source)
XLA Modules:
  0.0 69.0 jit_solution(17427558379405883933)
XLA Ops:
  0.0 2.0 %owner_lookup.1.x_ref = bf16[64,512]{1,0:T(8,128)(2,1)} custom-call(s32[64,512]{1,0:T(8,128)} %bitcast.7, s32[16,128]{1,0:T(8,128)} %bitcast.8), custom_call_target="tpu_custom_call" | custom-call | tf_op jit(solution)/shard_map/owner_lookup/pallas_call | solution.py:71
  2.0 13.5 %gather_gx.1 = bf16[8,64,512]{2,1,0:T(8,128)(2,1)} custom-call(bf16[64,512]{1,0:T(8,128)(2,1)} %owner_lookup.1.x_ref), custom_call_target="tpu_custom_call" | custom-call | tf_op jit(solution)/shard_map/gather_gx/pallas_call | solution.py:118
  15.5 12.2 %smooth.1 = (f32[64,72,512]{2,1,0:T(8,128)}, f32[4,2,72,128]{3,2,1,0:T(8,128)}) custom-call(bf16[512,512]{1,0:T(8,128)(2,1)} %bitcast.6, bf16[8,144,512]{2,1,0:T(8,128)(2,1)} %constant.4.clone.mx_ref, bf16[1,512,512]{2,1,0:T(8,128)(2,1)} %constant.5.clone.my_ref), custom_call_target="tpu_custom_call" | custom-call | tf_op jit(solution)/shard_map/smooth/pallas_call | solution.py:259
  27.7 14.4 %merge_fam.1.tops_ref = f32[4,2,72,128]{3,2,1,0:T(8,128)} custom-call(f32[4,2,72,128]{3,2,1,0:T(8,128)} %get-tuple-element.7.x_ref), custom_call_target="tpu_custom_call" | custom-call | tf_op jit(solution)/shard_map/merge_fam/pallas_call | solution.py:178
  42.1 26.9 %redistance.1 = f32[64,64,512]{2,1,0:T(8,128)} custom-call(f32[4,2,72,128]{3,2,1,0:T(8,128)} %merge_fam.1.tops_ref, f32[64,72,512]{2,1,0:T(8,128)} %get-tuple-element.8.u_ref), custom_call_target="tpu_custom_call" | custom-call | tf_op jit(solution)/shard_map/redistance/pallas_call | solution.py:346

commit v3 on v2

--- a/solution.py
+++ b/solution.py
@@ -39,15 +39,12 @@
 
 def ring_rows(x_local, count, parts):
     rows = x_local + HALO
-    out = []
-    for part in range(parts):
-        r = np.arange(rows)
-        x = part * x_local + np.where(r < x_local + HALO // 2, r, r - rows)
-        out.append(x % count)
-    return np.stack(out)
-
-
-def owner_kernel(labels_ref, table_ref, out_ref):
+    r = np.arange(rows).reshape(8, rows // 8).T.reshape(-1)
+    away = np.where(r < x_local + HALO // 2, r, r - rows)
+    return np.stack([(part * x_local + away) % count for part in range(parts)])
+
+
+def look_up(labels_ref, table_ref, out_ref):
     rows, cols = labels_ref.shape
     words = []
     for k in range(table_ref.shape[0] // 4):
@@ -67,16 +64,7 @@
         out_ref[:, c * LANES : (c + 1) * LANES] = acc.astype(jnp.float32).astype(out_ref.dtype)
 
 
-def owners(labels, table):
-    return pl.pallas_call(
-        owner_kernel,
-        out_shape=jax.ShapeDtypeStruct(labels.shape, jnp.bfloat16),
-        compiler_params=pltpu.CompilerParams(vmem_limit_bytes=VMEM),
-        name="owner_lookup",
-    )(labels, table)
-
-
-def gather_kernel(axis, size, x_ref, out_ref, send_sem, recv_sem, local_sem):
+def gather_kernel(axis, size, labels_ref, table_ref, out_ref, x_ref, send_sem, recv_sem, local_sem):
     me = lax.axis_index(axis)
     chips = size // 2
     chip, core = me // 2, lax.rem(me, 2)
@@ -85,6 +73,7 @@
     barrier = pltpu.get_barrier_semaphore()
     for device in [beside, *others]:
         pl.semaphore_signal(barrier, inc=1, device_id={axis: device}, device_id_type=MESH)
+    look_up(labels_ref, table_ref, x_ref)
     local = pltpu.make_async_copy(x_ref, out_ref.at[me], local_sem)
     local.start()
     pl.semaphore_wait(barrier, chips)
@@ -114,13 +103,14 @@
         copy.wait()
 
 
-def gathered(x, axis, size, collective_id):
+def gathered_owners(labels, table, axis, size, collective_id):
     return pl.pallas_call(
         functools.partial(gather_kernel, axis, size),
-        out_shape=jax.ShapeDtypeStruct((size, *x.shape), x.dtype),
-        in_specs=[pl.BlockSpec(memory_space=pltpu.VMEM)],
+        out_shape=jax.ShapeDtypeStruct((size, *labels.shape), jnp.bfloat16),
+        in_specs=[pl.BlockSpec(memory_space=pltpu.VMEM)] * 2,
         out_specs=pl.BlockSpec(memory_space=pltpu.VMEM),
         scratch_shapes=[
+            pltpu.VMEM(labels.shape, jnp.bfloat16),
             pltpu.SemaphoreType.DMA((size - 1,)),
             pltpu.SemaphoreType.DMA((size - 1,)),
             pltpu.SemaphoreType.DMA,
@@ -129,7 +119,7 @@
             collective_id=collective_id, has_side_effects=True, vmem_limit_bytes=VMEM
         ),
         name="gather_" + axis,
-    )(x)
+    )(labels, table)
 
 
 def merge_kernel(axis, size, x_ref, out_ref, recv_ref, send_sem, recv_sem, back_send, back_recv):
@@ -196,7 +186,7 @@
 
 def smooth_kernel(
     x_local, fam_local, group,
-    owner_ref, mx_ref, my_ref, u_ref, tops_ref, rel_ref, own_ref, t_ref,
+    owner_ref, mx_ref, my_ref, u_ref, tops_ref, rel_ref, own_ref, ring_ref, t_ref,
 ):
     step = pl.program_id(0)
     nx, ny = owner_ref.shape
@@ -206,15 +196,20 @@
 
     @pl.when(step == 0)
     def _():
-        own_ref[0:x_local, :] = owner_ref[
-            pl.ds(pl.multiple_of(x0, x_local), x_local), :
-        ].astype(jnp.float32)
+        mine = owner_ref[pl.ds(pl.multiple_of(x0, x_local), x_local), :].astype(jnp.float32)
         after = lax.rem(x0 + x_local, nx)
         before = lax.rem(x0 + nx - 16, nx)
         right = owner_ref[pl.ds(pl.multiple_of(after, 16), 16), :].astype(jnp.float32)[0:HALO]
         left = owner_ref[pl.ds(pl.multiple_of(before, 16), 16), :].astype(jnp.float32)[HALO:16]
         place = lax.broadcasted_iota(jnp.int32, (HALO, ny), 0)
-        own_ref[x_local:rows, :] = jnp.where(place < HALO // 2, right, left)
+        halo = jnp.where(place < HALO // 2, right, left)
+        strips = rows // 8
+        for c in range(ny // LANES):
+            cols = slice(c * LANES, (c + 1) * LANES)
+            ring_ref[c, 0:x_local, :] = mine[:, cols]
+            ring_ref[c, x_local:rows, :] = halo[:, cols]
+            for r in range(strips):
+                own_ref[8 * r : 8 * r + 8, cols] = ring_ref[c, pl.ds(r, 8, stride=strips), :]
         tops_ref[...] = jnp.full(tops_ref.shape, BIG, jnp.float32)
 
     shift = jnp.full((nx, ny), first.astype(jnp.float32), jnp.float32).astype(jnp.bfloat16)
@@ -275,6 +270,7 @@
         scratch_shapes=[
             pltpu.VMEM((nx, ny), jnp.bfloat16),
             pltpu.VMEM((rows, ny), jnp.float32),
+            pltpu.VMEM((ny // LANES, rows, LANES), jnp.float32),
             pltpu.VMEM((group * rows, ny), jnp.float32),
         ],
         compiler_params=pltpu.CompilerParams(vmem_limit_bytes=VMEM),
@@ -282,58 +278,89 @@
     )(owner, mx, my)
 
 
-def redistance_kernel(x_local, group, tops_ref, u_ref, out_ref, phi_ref, sig_ref, half_ref):
+def redistance_kernel(
+    x_local, group, tops_ref, u_ref, out_ref, first_ref, half_ref, phi_ref, order_ref, flag_ref
+):
     rows, ny = u_ref.shape[1:]
     chunks = ny // LANES
     strips = rows // 8
-
     per_piece = tops_ref.shape[2] // 8
+
+    def strip(r):
+        return slice(8 * r, 8 * r + 8)
+
+    def chunk(c):
+        return slice(c * LANES, (c + 1) * LANES)
+
+    peaks = [jnp.full((8, LANES), BIG, jnp.float32) for _ in range(group)]
+    for r in range(strips):
+        for c in range(chunks):
+            piece, place = tile_place(r * chunks + c, per_piece)
+            top1, top2 = tops_ref[piece, 0, place, :], tops_ref[piece, 1, place, :]
+            for j in range(group):
+                u = u_ref[j, strip(r), chunk(c)]
+                phi = scale_factor * (u - jnp.where(u >= top1, top2, top1))
+                first_ref[j, strip(r), chunk(c)] = phi
+                half_ref[j, strip(r), chunk(c)] = phi * (step_size * lax.rsqrt(phi * phi + 1.0))
+                peaks[j] = jnp.maximum(peaks[j], phi)
+    for j in range(group):
+        flag_ref[j] = (jnp.max(peaks[j]) > 0.0).astype(jnp.int32)
+
     lane = lax.broadcasted_iota(jnp.int32, (8, LANES), 1)
     is_first, is_last = lane == 0, lane == LANES - 1
 
-    def put(slot, r, c, value):
-        phi_ref[slot, c, 8 * r + HALO : 8 * r + HALO + 8, :] = value
-        if r == strips - 1:
-            phi_ref[slot, c, 0:HALO, :] = value
-
-    def one(j, carry):
-        for r in range(strips):
-            for c in range(chunks):
-                rs, cs = slice(8 * r, 8 * r + 8), slice(c * LANES, (c + 1) * LANES)
-                u = u_ref[j, rs, cs]
-                piece, place = tile_place(r * chunks + c, per_piece)
-                top1, top2 = tops_ref[piece, 0, place, :], tops_ref[piece, 1, place, :]
-                phi = scale_factor * (u - jnp.where(u >= top1, top2, top1))
-                put(0, r, c, phi)
-                sig_ref[c, rs, :] = jnp.where(phi > 0.0, 1.0, -1.0)
-                half_ref[c, rs, :] = phi * (step_size * lax.rsqrt(phi * phi + 1.0))
+    def sweeps(j, some_positive):
         for sweep in range(SWEEPS):
-            src, dst = sweep % 2, (sweep + 1) % 2
-            final = sweep == SWEEPS - 1
-            for r in range(x_local // 8 if final else strips):
-                rs = slice(8 * r, 8 * r + 8)
-                mid = [phi_ref[src, c, 8 * r + HALO : 8 * r + HALO + 8, :] for c in range(chunks)]
+            if sweep == 0:
+                src = first_ref.at[j]
+            else:
+                src = phi_ref.at[(sweep + 1) % 2]
+            dst = phi_ref.at[sweep % 2]
+
+            def load(r):
+                return [src[strip(r), chunk(c)] for c in range(chunks)]
+
+            bottom = [pltpu.roll(v, 1, 0) for v in load(strips - 1)]
+            top = [pltpu.roll(v, 7, 0) for v in load(0)]
+            low, mid = bottom, load(0)
+            for r in range(strips):
+                high = top if r == strips - 1 else load(r + 1)
                 to_right = [pltpu.roll(v, 1, 1) for v in mid]
                 to_left = [pltpu.roll(v, LANES - 1, 1) for v in mid]
                 for c in range(chunks):
-                    sig, half, centre = sig_ref[c, rs, :], half_ref[c, rs, :], mid[c]
+                    half, here = half_ref[j, strip(r), chunk(c)], mid[c]
                     y_low = jnp.where(is_first, to_right[c - 1], to_right[c])
                     y_high = jnp.where(is_last, to_left[(c + 1) % chunks], to_left[c])
-                    x_low = phi_ref[src, c, 8 * r + HALO - 1 : 8 * r + HALO + 7, :]
-                    if r == strips - 1:
-                        x_high = phi_ref[src, c, 1:9, :]
+                    if some_positive:
+                        sig = jnp.where(half > 0.0, 1.0, -1.0)
+                        size = here * sig
+                        gx = size - jnp.minimum(low[c] * sig, high[c] * sig)
+                        gy = size - jnp.minimum(y_low * sig, y_high * sig)
                     else:
-                        x_high = phi_ref[src, c, 8 * r + HALO + 1 : 8 * r + HALO + 9, :]
-                    here = centre * sig
-                    gx = jnp.maximum(here - jnp.minimum(x_low * sig, x_high * sig), 1e-18)
-                    gy = jnp.maximum(here - jnp.minimum(y_low * sig, y_high * sig), 1e-18)
+                        gx = jnp.maximum(low[c], high[c]) - here
+                        gy = jnp.maximum(y_low, y_high) - here
+                    gx, gy = jnp.maximum(gx, 1e-18), jnp.maximum(gy, 1e-18)
                     square = gx * gx + gy * gy
                     grad = square * lax.rsqrt(square)
-                    new = centre - half * (grad - 1.0)
-                    if final:
-                        out_ref[j, rs, c * LANES : (c + 1) * LANES] = new
+                    new = here - half * (grad - 1.0)
+                    if sweep == SWEEPS - 1:
+                        order_ref[c, pl.ds(r, 8, stride=strips), :] = new
                     else:
-                        put(dst, r, c, new)
+                        dst[strip(r), chunk(c)] = new
+                low, mid = mid, high
+        for r in range(x_local // 8):
+            for c in range(chunks):
+                out_ref[j, strip(r), chunk(c)] = order_ref[c, strip(r), :]
+
+    def one(j, carry):
+        @pl.when(flag_ref[j] == 0)
+        def _():
+            sweeps(j, False)
+
+        @pl.when(flag_ref[j] != 0)
+        def _():
+            sweeps(j, True)
+
         return carry
 
     lax.fori_loop(0, group, one, 0)
@@ -353,9 +380,11 @@
         ],
         out_specs=pl.BlockSpec((group, x_local, ny), lambda i: (i, 0, 0)),
         scratch_shapes=[
-            pltpu.VMEM((2, chunks, rows + HALO, LANES), jnp.float32),
+            pltpu.VMEM((group, rows, ny), jnp.float32),
+            pltpu.VMEM((group, rows, ny), jnp.float32),
+            pltpu.VMEM((2, rows, ny), jnp.float32),
             pltpu.VMEM((chunks, rows, LANES), jnp.float32),
-            pltpu.VMEM((chunks, rows, LANES), jnp.float32),
+            pltpu.SMEM((group,), jnp.int32),
         ],
         compiler_params=pltpu.CompilerParams(vmem_limit_bytes=VMEM),
         name="redistance",
@@ -368,8 +397,8 @@
     assert nz == 1
     nx = x_local * parts
     fam_local = F // fams
-    owner = owners(labels[0], family_of_grain.reshape(-1, LANES))
-    owner = gathered(owner, "gx", parts, 0).reshape(nx, ny)
+    table = family_of_grain.reshape(-1, LANES)
+    owner = gathered_owners(labels[0], table, "gx", parts, 0).reshape(nx, ny)
     u, tops = smoothed(owner, mx, my, x_local, fam_local, fams)
     tops = merged(tops, "fam", fams, 1)
     return redistanced(tops, u, x_local)[:, None]

time: 69.3 us -> 72 us (1.039)
  Pallas kernels: 69 us -> 71.7 us
    pallas_call x1, Pallas kernels: 26.9 us -> 31.5 us  [redistanced(): pl.pallas_call(functools.partial(redistance_kernel, x_local, group), grid...]
    pallas_call x2 -> x1, Pallas kernels: 15.5 us -> 13.6 us  [gathered_owners(): pl.pallas_call(functools.partial(gather_kernel, axis, size), out_shape=ja...]
where the time goes in v3:
time: 72 us; the launch traced here: 71.7 us
  Pallas kernels  71.7 us (100%)
    pallas_call x1, Pallas kernels, redistanced(): pl.pallas_call(functools.partial(redistance_kernel, x_local, group), grid...  31.5 us
    pallas_call x1, Pallas kernels, merged(): pl.pallas_call(functools.partial(merge_kernel, axis, size), out_shape=jax...  14.4 us
    pallas_call x1, Pallas kernels, gathered_owners(): pl.pallas_call(functools.partial(gather_kernel, axis, size), out_shape=ja...  13.6 us
    pallas_call x1, Pallas kernels, smoothed(): pl.pallas_call(functools.partial(smooth_kernel, x_local, fam_local, group...  12.2 us

profile of v3, /device:TPU:0, one launch (start us, length us, event | category | flops | bytes accessed | tf_op | source)
XLA Modules:
  0.0 71.7 jit_solution(1436261221456791979)
XLA Ops:
  0.0 13.6 %gather_gx.1 = bf16[8,64,512]{2,1,0:T(8,128)(2,1)} custom-call(s32[64,512]{1,0:T(8,128)} %bitcast.7, s32[16,128]{1,0:T(8,128)} %bitcast.8), custom_call_target="tpu_custom_call" | custom-call | tf_op jit(solution)/shard_map/gather_gx/pallas_call | solution.py:107
  13.6 12.2 %smooth.1 = (f32[64,72,512]{2,1,0:T(8,128)}, f32[4,2,72,128]{3,2,1,0:T(8,128)}) custom-call(bf16[512,512]{1,0:T(8,128)(2,1)} %bitcast.6, bf16[8,144,512]{2,1,0:T(8,128)(2,1)} %constant.4.clone.mx_ref, bf16[1,512,512]{2,1,0:T(8,128)(2,1)} %constant.5.clone.my_ref), custom_call_target="tpu_custom_call" | custom-call | tf_op jit(solution)/shard_map/smooth/pallas_call | solution.py:254
  25.8 14.4 %merge_fam.1.tops_ref = f32[4,2,72,128]{3,2,1,0:T(8,128)} custom-call(f32[4,2,72,128]{3,2,1,0:T(8,128)} %get-tuple-element.7.x_ref), custom_call_target="tpu_custom_call" | custom-call | tf_op jit(solution)/shard_map/merge_fam/pallas_call | solution.py:168
  40.2 31.5 %redistance.1 = f32[64,64,512]{2,1,0:T(8,128)} custom-call(f32[4,2,72,128]{3,2,1,0:T(8,128)} %merge_fam.1.tops_ref, f32[64,72,512]{2,1,0:T(8,128)} %get-tuple-element.8.u_ref), custom_call_target="tpu_custom_call" | custom-call | tf_op jit(solution)/shard_map/redistance/pallas_call | solution.py:373

commit v4 on v3

--- a/solution.py
+++ b/solution.py
@@ -39,7 +39,7 @@
 
 def ring_rows(x_local, count, parts):
     rows = x_local + HALO
-    r = np.arange(rows).reshape(8, rows // 8).T.reshape(-1)
+    r = np.arange(rows)
     away = np.where(r < x_local + HALO // 2, r, r - rows)
     return np.stack([(part * x_local + away) % count for part in range(parts)])
 
@@ -186,7 +186,7 @@
 
 def smooth_kernel(
     x_local, fam_local, group,
-    owner_ref, mx_ref, my_ref, u_ref, tops_ref, rel_ref, own_ref, ring_ref, t_ref,
+    owner_ref, mx_ref, my_ref, u_ref, tops_ref, rel_ref, own_ref, t_ref,
 ):
     step = pl.program_id(0)
     nx, ny = owner_ref.shape
@@ -202,14 +202,8 @@
         right = owner_ref[pl.ds(pl.multiple_of(after, 16), 16), :].astype(jnp.float32)[0:HALO]
         left = owner_ref[pl.ds(pl.multiple_of(before, 16), 16), :].astype(jnp.float32)[HALO:16]
         place = lax.broadcasted_iota(jnp.int32, (HALO, ny), 0)
-        halo = jnp.where(place < HALO // 2, right, left)
-        strips = rows // 8
-        for c in range(ny // LANES):
-            cols = slice(c * LANES, (c + 1) * LANES)
-            ring_ref[c, 0:x_local, :] = mine[:, cols]
-            ring_ref[c, x_local:rows, :] = halo[:, cols]
-            for r in range(strips):
-                own_ref[8 * r : 8 * r + 8, cols] = ring_ref[c, pl.ds(r, 8, stride=strips), :]
+        own_ref[0:x_local, :] = mine
+        own_ref[x_local:rows, :] = jnp.where(place < HALO // 2, right, left)
         tops_ref[...] = jnp.full(tops_ref.shape, BIG, jnp.float32)
 
     shift = jnp.full((nx, ny), first.astype(jnp.float32), jnp.float32).astype(jnp.bfloat16)
@@ -270,7 +264,6 @@
         scratch_shapes=[
             pltpu.VMEM((nx, ny), jnp.bfloat16),
             pltpu.VMEM((rows, ny), jnp.float32),
-            pltpu.VMEM((ny // LANES, rows, LANES), jnp.float32),
             pltpu.VMEM((group * rows, ny), jnp.float32),
         ],
         compiler_params=pltpu.CompilerParams(vmem_limit_bytes=VMEM),
@@ -279,7 +272,7 @@
 
 
 def redistance_kernel(
-    x_local, group, tops_ref, u_ref, out_ref, first_ref, half_ref, phi_ref, order_ref, flag_ref
+    x_local, group, tops_ref, u_ref, out_ref, half_ref, first_ref, phi_ref, flag_ref
 ):
     rows, ny = u_ref.shape[1:]
     chunks = ny // LANES
@@ -291,6 +284,11 @@
 
     def chunk(c):
         return slice(c * LANES, (c + 1) * LANES)
+
+    def put(ref, r, c, value):
+        ref[c, 8 * r + HALO : 8 * r + HALO + 8, :] = value
+        if r == strips - 1:
+            ref[c, 0:HALO, :] = value
 
     peaks = [jnp.full((8, LANES), BIG, jnp.float32) for _ in range(group)]
     for r in range(strips):
@@ -300,7 +298,7 @@
             for j in range(group):
                 u = u_ref[j, strip(r), chunk(c)]
                 phi = scale_factor * (u - jnp.where(u >= top1, top2, top1))
-                first_ref[j, strip(r), chunk(c)] = phi
+                put(first_ref.at[j], r, c, phi)
                 half_ref[j, strip(r), chunk(c)] = phi * (step_size * lax.rsqrt(phi * phi + 1.0))
                 peaks[j] = jnp.maximum(peaks[j], phi)
     for j in range(group):
@@ -317,40 +315,38 @@
                 src = phi_ref.at[(sweep + 1) % 2]
             dst = phi_ref.at[sweep % 2]
 
-            def load(r):
-                return [src[strip(r), chunk(c)] for c in range(chunks)]
-
-            bottom = [pltpu.roll(v, 1, 0) for v in load(strips - 1)]
-            top = [pltpu.roll(v, 7, 0) for v in load(0)]
-            low, mid = bottom, load(0)
-            for r in range(strips):
-                high = top if r == strips - 1 else load(r + 1)
+            def load(r, c, shift):
+                start = 8 * r + HALO + shift
+                if r == strips - 1 and shift > 0:
+                    start = shift
+                return src[c, start : start + 8, :]
+
+            final = sweep == SWEEPS - 1
+            for r in range(x_local // 8 if final else strips):
+                mid = [load(r, c, 0) for c in range(chunks)]
                 to_right = [pltpu.roll(v, 1, 1) for v in mid]
                 to_left = [pltpu.roll(v, LANES - 1, 1) for v in mid]
                 for c in range(chunks):
                     half, here = half_ref[j, strip(r), chunk(c)], mid[c]
+                    x_low, x_high = load(r, c, -1), load(r, c, 1)
                     y_low = jnp.where(is_first, to_right[c - 1], to_right[c])
                     y_high = jnp.where(is_last, to_left[(c + 1) % chunks], to_left[c])
                     if some_positive:
                         sig = jnp.where(half > 0.0, 1.0, -1.0)
                         size = here * sig
-                        gx = size - jnp.minimum(low[c] * sig, high[c] * sig)
+                        gx = size - jnp.minimum(x_low * sig, x_high * sig)
                         gy = size - jnp.minimum(y_low * sig, y_high * sig)
                     else:
-                        gx = jnp.maximum(low[c], high[c]) - here
+                        gx = jnp.maximum(x_low, x_high) - here
                         gy = jnp.maximum(y_low, y_high) - here
                     gx, gy = jnp.maximum(gx, 1e-18), jnp.maximum(gy, 1e-18)
                     square = gx * gx + gy * gy
                     grad = square * lax.rsqrt(square)
                     new = here - half * (grad - 1.0)
-                    if sweep == SWEEPS - 1:
-                        order_ref[c, pl.ds(r, 8, stride=strips), :] = new
+                    if final:
+                        out_ref[j, strip(r), chunk(c)] = new
                     else:
-                        dst[strip(r), chunk(c)] = new
-                low, mid = mid, high
-        for r in range(x_local // 8):
-            for c in range(chunks):
-                out_ref[j, strip(r), chunk(c)] = order_ref[c, strip(r), :]
+                        put(dst, r, c, new)
 
     def one(j, carry):
         @pl.when(flag_ref[j] == 0)
@@ -381,9 +377,8 @@
         out_specs=pl.BlockSpec((group, x_local, ny), lambda i: (i, 0, 0)),
         scratch_shapes=[
             pltpu.VMEM((group, rows, ny), jnp.float32),
-            pltpu.VMEM((group, rows, ny), jnp.float32),
-            pltpu.VMEM((2, rows, ny), jnp.float32),
-            pltpu.VMEM((chunks, rows, LANES), jnp.float32),
+            pltpu.VMEM((group, chunks, rows + HALO, LANES), jnp.float32),
+            pltpu.VMEM((2, chunks, rows + HALO, LANES), jnp.float32),
             pltpu.SMEM((group,), jnp.int32),
         ],
         compiler_params=pltpu.CompilerParams(vmem_limit_bytes=VMEM),

time: 72 us -> 71.1 us (0.987)
  Pallas kernels: 71.7 us -> 70.8 us
    pallas_call x1, Pallas kernels: 31.5 us -> 30.7 us  [redistanced(): pl.pallas_call(functools.partial(redistance_kernel, x_local, group), grid...]
where the time goes in v4:
time: 71.1 us; the launch traced here: 70.9 us
  Pallas kernels  70.8 us (100%)
    pallas_call x1, Pallas kernels, redistanced(): pl.pallas_call(functools.partial(redistance_kernel, x_local, group), grid...  30.7 us
    pallas_call x1, Pallas kernels, merged(): pl.pallas_call(functools.partial(merge_kernel, axis, size), out_shape=jax...  14.4 us
    pallas_call x1, Pallas kernels, gathered_owners(): pl.pallas_call(functools.partial(gather_kernel, axis, size), out_shape=ja...  13.6 us
    pallas_call x1, Pallas kernels, smoothed(): pl.pallas_call(functools.partial(smooth_kernel, x_local, fam_local, group...  12.2 us

profile of v4, /device:TPU:0, one launch (start us, length us, event | category | flops | bytes accessed | tf_op | source)
XLA Modules:
  0.0 70.9 jit_solution(4524087211781711982)
XLA Ops:
  0.0 13.6 %gather_gx.1 = bf16[8,64,512]{2,1,0:T(8,128)(2,1)} custom-call(s32[64,512]{1,0:T(8,128)} %bitcast.7, s32[16,128]{1,0:T(8,128)} %bitcast.8), custom_call_target="tpu_custom_call" | custom-call | tf_op jit(solution)/shard_map/gather_gx/pallas_call | solution.py:107
  13.6 12.2 %smooth.1 = (f32[64,72,512]{2,1,0:T(8,128)}, f32[4,2,72,128]{3,2,1,0:T(8,128)}) custom-call(bf16[512,512]{1,0:T(8,128)(2,1)} %bitcast.6, bf16[8,144,512]{2,1,0:T(8,128)(2,1)} %constant.4.clone.mx_ref, bf16[1,512,512]{2,1,0:T(8,128)(2,1)} %constant.5.clone.my_ref), custom_call_target="tpu_custom_call" | custom-call | tf_op jit(solution)/shard_map/smooth/pallas_call | solution.py:248
  25.8 14.4 %merge_fam.1.tops_ref = f32[4,2,72,128]{3,2,1,0:T(8,128)} custom-call(f32[4,2,72,128]{3,2,1,0:T(8,128)} %get-tuple-element.7.x_ref), custom_call_target="tpu_custom_call" | custom-call | tf_op jit(solution)/shard_map/merge_fam/pallas_call | solution.py:168
  40.2 30.7 %redistance.1 = f32[64,64,512]{2,1,0:T(8,128)} custom-call(f32[4,2,72,128]{3,2,1,0:T(8,128)} %merge_fam.1.tops_ref, f32[64,72,512]{2,1,0:T(8,128)} %get-tuple-element.8.u_ref), custom_call_target="tpu_custom_call" | custom-call | tf_op jit(solution)/shard_map/redistance/pallas_call | solution.py:369

commit v5 on v2

--- a/solution.py
+++ b/solution.py
@@ -39,15 +39,12 @@
 
 def ring_rows(x_local, count, parts):
     rows = x_local + HALO
-    out = []
-    for part in range(parts):
-        r = np.arange(rows)
-        x = part * x_local + np.where(r < x_local + HALO // 2, r, r - rows)
-        out.append(x % count)
-    return np.stack(out)
-
-
-def owner_kernel(labels_ref, table_ref, out_ref):
+    r = np.arange(rows)
+    away = np.where(r < x_local + HALO // 2, r, r - rows)
+    return np.stack([(part * x_local + away) % count for part in range(parts)])
+
+
+def look_up(labels_ref, table_ref, out_ref):
     rows, cols = labels_ref.shape
     words = []
     for k in range(table_ref.shape[0] // 4):
@@ -67,16 +64,7 @@
         out_ref[:, c * LANES : (c + 1) * LANES] = acc.astype(jnp.float32).astype(out_ref.dtype)
 
 
-def owners(labels, table):
-    return pl.pallas_call(
-        owner_kernel,
-        out_shape=jax.ShapeDtypeStruct(labels.shape, jnp.bfloat16),
-        compiler_params=pltpu.CompilerParams(vmem_limit_bytes=VMEM),
-        name="owner_lookup",
-    )(labels, table)
-
-
-def gather_kernel(axis, size, x_ref, out_ref, send_sem, recv_sem, local_sem):
+def gather_kernel(axis, size, labels_ref, table_ref, out_ref, x_ref, send_sem, recv_sem, local_sem):
     me = lax.axis_index(axis)
     chips = size // 2
     chip, core = me // 2, lax.rem(me, 2)
@@ -85,6 +73,7 @@
     barrier = pltpu.get_barrier_semaphore()
     for device in [beside, *others]:
         pl.semaphore_signal(barrier, inc=1, device_id={axis: device}, device_id_type=MESH)
+    look_up(labels_ref, table_ref, x_ref)
     local = pltpu.make_async_copy(x_ref, out_ref.at[me], local_sem)
     local.start()
     pl.semaphore_wait(barrier, chips)
@@ -114,13 +103,14 @@
         copy.wait()
 
 
-def gathered(x, axis, size, collective_id):
+def gathered_owners(labels, table, axis, size, collective_id):
     return pl.pallas_call(
         functools.partial(gather_kernel, axis, size),
-        out_shape=jax.ShapeDtypeStruct((size, *x.shape), x.dtype),
-        in_specs=[pl.BlockSpec(memory_space=pltpu.VMEM)],
+        out_shape=jax.ShapeDtypeStruct((size, *labels.shape), jnp.bfloat16),
+        in_specs=[pl.BlockSpec(memory_space=pltpu.VMEM)] * 2,
         out_specs=pl.BlockSpec(memory_space=pltpu.VMEM),
         scratch_shapes=[
+            pltpu.VMEM(labels.shape, jnp.bfloat16),
             pltpu.SemaphoreType.DMA((size - 1,)),
             pltpu.SemaphoreType.DMA((size - 1,)),
             pltpu.SemaphoreType.DMA,
@@ -129,16 +119,23 @@
             collective_id=collective_id, has_side_effects=True, vmem_limit_bytes=VMEM
         ),
         name="gather_" + axis,
-    )(x)
-
-
-def merge_kernel(axis, size, x_ref, out_ref, recv_ref, send_sem, recv_sem, back_send, back_recv):
+    )(labels, table)
+
+
+def peers(axis, size):
     me = lax.axis_index(axis)
-    others = [lax.rem(me + k, size) for k in range(1, size)]
+    return me, [lax.rem(me + k, size) for k in range(1, size)]
+
+
+def greet(axis, size):
     barrier = pltpu.get_barrier_semaphore()
-    for device in others:
+    for device in peers(axis, size)[1]:
         pl.semaphore_signal(barrier, inc=1, device_id={axis: device}, device_id_type=MESH)
-    pl.semaphore_wait(barrier, size - 1)
+
+
+def merge(axis, size, x_ref, out_ref, recv_ref, send_sem, recv_sem, back_send, back_recv):
+    me, others = peers(axis, size)
+    pl.semaphore_wait(pltpu.get_barrier_semaphore(), size - 1)
 
     def send(src, dst, sems, k, device):
         copy = pltpu.make_async_remote_copy(
@@ -174,21 +171,6 @@
         copy.wait()
 
 
-def merged(x, axis, size, collective_id):
-    return pl.pallas_call(
-        functools.partial(merge_kernel, axis, size),
-        out_shape=jax.ShapeDtypeStruct(x.shape, x.dtype),
-        in_specs=[pl.BlockSpec(memory_space=pltpu.VMEM)],
-        out_specs=pl.BlockSpec(memory_space=pltpu.VMEM),
-        scratch_shapes=[pltpu.VMEM((size - 1, *x.shape[1:]), x.dtype)]
-        + [pltpu.SemaphoreType.DMA((size - 1,))] * 4,
-        compiler_params=pltpu.CompilerParams(
-            collective_id=collective_id, has_side_effects=True, vmem_limit_bytes=VMEM
-        ),
-        name="merge_" + axis,
-    )(x)
-
-
 def tile_place(k, per_piece):
     row = 8 * (k % per_piece)
     return k // per_piece, slice(row, row + 8)
@@ -196,7 +178,7 @@
 
 def smooth_kernel(
     x_local, fam_local, group,
-    owner_ref, mx_ref, my_ref, u_ref, tops_ref, rel_ref, own_ref, t_ref,
+    owner_ref, mx_ref, my_ref, u_ref, all_ref, rel_ref, own_ref, t_ref, tops_ref, *exchange,
 ):
     step = pl.program_id(0)
     nx, ny = owner_ref.shape
@@ -206,14 +188,14 @@
 
     @pl.when(step == 0)
     def _():
-        own_ref[0:x_local, :] = owner_ref[
-            pl.ds(pl.multiple_of(x0, x_local), x_local), :
-        ].astype(jnp.float32)
+        greet("fam", tops_ref.shape[0])
+        mine = owner_ref[pl.ds(pl.multiple_of(x0, x_local), x_local), :].astype(jnp.float32)
         after = lax.rem(x0 + x_local, nx)
         before = lax.rem(x0 + nx - 16, nx)
         right = owner_ref[pl.ds(pl.multiple_of(after, 16), 16), :].astype(jnp.float32)[0:HALO]
         left = owner_ref[pl.ds(pl.multiple_of(before, 16), 16), :].astype(jnp.float32)[HALO:16]
         place = lax.broadcasted_iota(jnp.int32, (HALO, ny), 0)
+        own_ref[0:x_local, :] = mine
         own_ref[x_local:rows, :] = jnp.where(place < HALO // 2, right, left)
         tops_ref[...] = jnp.full(tops_ref.shape, BIG, jnp.float32)
 
@@ -249,6 +231,11 @@
             tops_ref[piece, 0, place, :] = high
             tops_ref[piece, 1, place, :] = second
 
+    @pl.when(step == pl.num_programs(0) - 1)
+    def _():
+        merge("fam", tops_ref.shape[0], tops_ref, *exchange)
+        all_ref[...] = exchange[0][...]
+
 
 def smoothed(owner, mx, my, x_local, fam_local, fams):
     nx, ny = owner.shape
@@ -276,8 +263,14 @@
             pltpu.VMEM((nx, ny), jnp.bfloat16),
             pltpu.VMEM((rows, ny), jnp.float32),
             pltpu.VMEM((group * rows, ny), jnp.float32),
-        ],
-        compiler_params=pltpu.CompilerParams(vmem_limit_bytes=VMEM),
+            pltpu.VMEM(pieces, jnp.float32),
+            pltpu.VMEM(pieces, jnp.float32),
+            pltpu.VMEM((fams - 1, *pieces[1:]), jnp.float32),
+        ]
+        + [pltpu.SemaphoreType.DMA((fams - 1,))] * 4,
+        compiler_params=pltpu.CompilerParams(
+            collective_id=1, has_side_effects=True, vmem_limit_bytes=VMEM
+        ),
         name="smooth",
     )(owner, mx, my)
 
@@ -368,10 +361,9 @@
     assert nz == 1
     nx = x_local * parts
     fam_local = F // fams
-    owner = owners(labels[0], family_of_grain.reshape(-1, LANES))
-    owner = gathered(owner, "gx", parts, 0).reshape(nx, ny)
+    table = family_of_grain.reshape(-1, LANES)
+    owner = gathered_owners(labels[0], table, "gx", parts, 0).reshape(nx, ny)
     u, tops = smoothed(owner, mx, my, x_local, fam_local, fams)
-    tops = merged(tops, "fam", fams, 1)
     return redistanced(tops, u, x_local)[:, None]
 
 

time: 69.3 us -> 64.3 us (0.928)
  Pallas kernels: 69 us -> 64.1 us
    pallas_call x3 -> x1, Pallas kernels: 29.9 us -> 13.6 us  [gathered_owners(): pl.pallas_call(functools.partial(gather_kernel, axis, size), out_shape=ja...]
    pallas_call x1, Pallas kernels: 12.2 us -> 23.7 us  [smoothed(): pl.pallas_call(functools.partial(smooth_kernel, x_local, fam_local, group...]
where the time goes in v5:
time: 64.3 us; the launch traced here: 64.2 us
  Pallas kernels  64.1 us (100%)
    pallas_call x1, Pallas kernels, redistanced(): pl.pallas_call(functools.partial(redistance_kernel, x_local, group), grid...  26.9 us
    pallas_call x1, Pallas kernels, smoothed(): pl.pallas_call(functools.partial(smooth_kernel, x_local, fam_local, group...  23.7 us
    pallas_call x1, Pallas kernels, gathered_owners(): pl.pallas_call(functools.partial(gather_kernel, axis, size), out_shape=ja...  13.6 us

profile of v5, /device:TPU:0, one launch (start us, length us, event | category | flops | bytes accessed | tf_op | source)
XLA Modules:
  0.0 64.2 jit_solution(3220296538623884433)
XLA Ops:
  0.0 13.6 %gather_gx.1 = bf16[8,64,512]{2,1,0:T(8,128)(2,1)} custom-call(s32[64,512]{1,0:T(8,128)} %bitcast.7, s32[16,128]{1,0:T(8,128)} %bitcast.8), custom_call_target="tpu_custom_call" | custom-call | tf_op jit(solution)/shard_map/gather_gx/pallas_call | solution.py:107
  13.6 23.7 %smooth.1 = (f32[64,72,512]{2,1,0:T(8,128)}, f32[4,2,72,128]{3,2,1,0:T(8,128)}) custom-call(bf16[512,512]{1,0:T(8,128)(2,1)} %bitcast.6, bf16[8,144,512]{2,1,0:T(8,128)(2,1)} %constant.4.clone.mx_ref, bf16[1,512,512]{2,1,0:T(8,128)(2,1)} %constant.5.clone.my_ref), custom_call_target="tpu_custom_call" | custom-call | tf_op jit(solution)/shard_map/smooth/pallas_call | solution.py:246
  37.2 26.9 %redistance.1 = f32[64,64,512]{2,1,0:T(8,128)} custom-call(f32[4,2,72,128]{3,2,1,0:T(8,128)} %get-tuple-element.7.tops_ref, f32[64,72,512]{2,1,0:T(8,128)} %get-tuple-element.8.u_ref), custom_call_target="tpu_custom_call" | custom-call | tf_op jit(solution)/shard_map/redistance/pallas_call | solution.py:339

commit v6 on v5

--- a/solution.py
+++ b/solution.py
@@ -42,6 +42,13 @@
     r = np.arange(rows)
     away = np.where(r < x_local + HALO // 2, r, r - rows)
     return np.stack([(part * x_local + away) % count for part in range(parts)])
+
+
+def spread_columns(count):
+    place = np.arange(count)
+    spread = (place % LANES) * (count // LANES) + place // LANES
+    to_spread = (np.arange(count)[:, None] == spread[None]).astype(ml_dtypes.bfloat16)
+    return spread, to_spread
 
 
 def look_up(labels_ref, table_ref, out_ref):
@@ -178,7 +185,7 @@
 
 def smooth_kernel(
     x_local, fam_local, group,
-    owner_ref, mx_ref, my_ref, u_ref, all_ref, rel_ref, own_ref, t_ref, tops_ref, *exchange,
+    owner_ref, mx_ref, my_ref, spread_ref, u_ref, all_ref, rel_ref, own_ref, t_ref, tops_ref, *exchange,
 ):
     step = pl.program_id(0)
     nx, ny = owner_ref.shape
@@ -197,6 +204,9 @@
         place = lax.broadcasted_iota(jnp.int32, (HALO, ny), 0)
         own_ref[0:x_local, :] = mine
         own_ref[x_local:rows, :] = jnp.where(place < HALO // 2, right, left)
+        own_ref[...] = jnp.dot(
+            own_ref[...].astype(jnp.bfloat16), spread_ref[...], preferred_element_type=jnp.float32
+        )
         tops_ref[...] = jnp.full(tops_ref.shape, BIG, jnp.float32)
 
     shift = jnp.full((nx, ny), first.astype(jnp.float32), jnp.float32).astype(jnp.bfloat16)
@@ -237,7 +247,7 @@
         all_ref[...] = exchange[0][...]
 
 
-def smoothed(owner, mx, my, x_local, fam_local, fams):
+def smoothed(owner, mx, my, spread, x_local, fam_local, fams):
     nx, ny = owner.shape
     rows = x_local + HALO
     group = min(8, fam_local)
@@ -254,6 +264,7 @@
             pl.BlockSpec((nx, ny), lambda i: (0, 0)),
             pl.BlockSpec((1, *mx.shape[1:]), lambda i: (lax.axis_index("gx"), 0, 0)),
             pl.BlockSpec(my.shape, lambda i: (0, 0, 0)),
+            pl.BlockSpec(spread.shape, lambda i: (0, 0)),
         ],
         out_specs=(
             pl.BlockSpec((group, rows, ny), lambda i: (i, 0, 0)),
@@ -272,17 +283,24 @@
             collective_id=1, has_side_effects=True, vmem_limit_bytes=VMEM
         ),
         name="smooth",
-    )(owner, mx, my)
-
-
-def redistance_kernel(x_local, group, tops_ref, u_ref, out_ref, phi_ref, sig_ref, half_ref):
+    )(owner, mx, my, spread)
+
+
+def redistance_kernel(
+    x_local, group, tops_ref, u_ref, back_ref, out_ref, phi_ref, sig_ref, half_ref, done_ref
+):
     rows, ny = u_ref.shape[1:]
     chunks = ny // LANES
     strips = rows // 8
 
     per_piece = tops_ref.shape[2] // 8
-    lane = lax.broadcasted_iota(jnp.int32, (8, LANES), 1)
-    is_first, is_last = lane == 0, lane == LANES - 1
+    def put_back(j):
+        done = done_ref[...]
+        high = done.astype(jnp.bfloat16)
+        low = (done - high.astype(jnp.float32)).astype(jnp.bfloat16)
+        both = jnp.concatenate([high, low], axis=0)
+        both = jnp.dot(both, back_ref[...], preferred_element_type=jnp.float32)
+        out_ref[j] = both[:x_local] + both[x_local:]
 
     def put(slot, r, c, value):
         phi_ref[slot, c, 8 * r + HALO : 8 * r + HALO + 8, :] = value
@@ -290,6 +308,7 @@
             phi_ref[slot, c, 0:HALO, :] = value
 
     def one(j, carry):
+        put_back(jnp.maximum(j - 1, 0))
         for r in range(strips):
             for c in range(chunks):
                 rs, cs = slice(8 * r, 8 * r + 8), slice(c * LANES, (c + 1) * LANES)
@@ -306,12 +325,10 @@
             for r in range(x_local // 8 if final else strips):
                 rs = slice(8 * r, 8 * r + 8)
                 mid = [phi_ref[src, c, 8 * r + HALO : 8 * r + HALO + 8, :] for c in range(chunks)]
-                to_right = [pltpu.roll(v, 1, 1) for v in mid]
-                to_left = [pltpu.roll(v, LANES - 1, 1) for v in mid]
+                around = [pltpu.roll(mid[-1], 1, 1), *mid, pltpu.roll(mid[0], LANES - 1, 1)]
                 for c in range(chunks):
                     sig, half, centre = sig_ref[c, rs, :], half_ref[c, rs, :], mid[c]
-                    y_low = jnp.where(is_first, to_right[c - 1], to_right[c])
-                    y_high = jnp.where(is_last, to_left[(c + 1) % chunks], to_left[c])
+                    y_low, y_high = around[c], around[c + 2]
                     x_low = phi_ref[src, c, 8 * r + HALO - 1 : 8 * r + HALO + 7, :]
                     if r == strips - 1:
                         x_high = phi_ref[src, c, 1:9, :]
@@ -324,15 +341,16 @@
                     grad = square * lax.rsqrt(square)
                     new = centre - half * (grad - 1.0)
                     if final:
-                        out_ref[j, rs, c * LANES : (c + 1) * LANES] = new
+                        done_ref[rs, c * LANES : (c + 1) * LANES] = new
                     else:
                         put(dst, r, c, new)
         return carry
 
     lax.fori_loop(0, group, one, 0)
-
-
-def redistanced(tops, u, x_local):
+    put_back(group - 1)
+
+
+def redistanced(tops, u, back, x_local):
     fam_local, rows, ny = u.shape
     group = min(8, fam_local)
     chunks = ny // LANES
@@ -343,19 +361,21 @@
         in_specs=[
             pl.BlockSpec(tops.shape, lambda i: (0, 0, 0, 0)),
             pl.BlockSpec((group, rows, ny), lambda i: (i, 0, 0)),
+            pl.BlockSpec(back.shape, lambda i: (0, 0)),
         ],
         out_specs=pl.BlockSpec((group, x_local, ny), lambda i: (i, 0, 0)),
         scratch_shapes=[
             pltpu.VMEM((2, chunks, rows + HALO, LANES), jnp.float32),
             pltpu.VMEM((chunks, rows, LANES), jnp.float32),
             pltpu.VMEM((chunks, rows, LANES), jnp.float32),
+            pltpu.VMEM((x_local, ny), jnp.float32),
         ],
         compiler_params=pltpu.CompilerParams(vmem_limit_bytes=VMEM),
         name="redistance",
-    )(tops, u)
-
-
-def body(labels, family_of_grain, mx, my):
+    )(tops, u, back)
+
+
+def body(labels, family_of_grain, mx, my, spread, back):
     parts, fams = lax.axis_size("gx"), lax.axis_size("fam")
     nz, x_local, ny = labels.shape
     assert nz == 1
@@ -363,8 +383,8 @@
     fam_local = F // fams
     table = family_of_grain.reshape(-1, LANES)
     owner = gathered_owners(labels[0], table, "gx", parts, 0).reshape(nx, ny)
-    u, tops = smoothed(owner, mx, my, x_local, fam_local, fams)
-    return redistanced(tops, u, x_local)[:, None]
+    u, tops = smoothed(owner, mx, my, spread, x_local, fam_local, fams)
+    return redistanced(tops, u, back, x_local)[:, None]
 
 
 def solution(mesh):
@@ -374,14 +394,17 @@
         high, low = smoothing(nx)
         rows = ring_rows(nx // parts, nx, parts)
         mx = jnp.asarray(np.concatenate([high[rows], low[rows]], axis=1))
-        my = jnp.asarray(smoothing(ny)[0][None])
+        order, spread = spread_columns(ny)
+        my = jnp.asarray(smoothing(ny)[0][None, :, order])
         mapped = jax.shard_map(
             body,
             mesh=mesh,
-            in_specs=(P(None, "gx", None), P(), P(), P()),
+            in_specs=(P(None, "gx", None), P(), P(), P(), P(), P()),
             out_specs=P("fam", None, "gx", None),
             check_vma=False,
         )
-        return mapped(labels, family_of_grain, mx, my)
+        return mapped(
+            labels, family_of_grain, mx, my, jnp.asarray(spread), jnp.asarray(spread.T)
+        )
 
     return run

time: 64.3 us -> 68.2 us (1.061)
  Pallas kernels: 64.1 us -> 68 us
    pallas_call x1, Pallas kernels: 26.9 us -> 30.4 us  [redistanced(): pl.pallas_call(functools.partial(redistance_kernel, x_local, group), grid...]
where the time goes in v6:
time: 68.2 us; the launch traced here: 68 us
  Pallas kernels  68 us (100%)
    pallas_call x1, Pallas kernels, redistanced(): pl.pallas_call(functools.partial(redistance_kernel, x_local, group), grid...  30.4 us
    pallas_call x1, Pallas kernels, smoothed(): pl.pallas_call(functools.partial(smooth_kernel, x_local, fam_local, group...  24 us
    pallas_call x1, Pallas kernels, gathered_owners(): pl.pallas_call(functools.partial(gather_kernel, axis, size), out_shape=ja...  13.6 us

profile of v6, /device:TPU:0, one launch (start us, length us, event | category | flops | bytes accessed | tf_op | source)
XLA Modules:
  0.0 68.0 jit_solution(14736073265171724802)
XLA Ops:
  0.0 13.6 %gather_gx.1 = bf16[8,64,512]{2,1,0:T(8,128)(2,1)} custom-call(s32[64,512]{1,0:T(8,128)} %bitcast.7, s32[16,128]{1,0:T(8,128)} %bitcast.8), custom_call_target="tpu_custom_call" | custom-call | tf_op jit(solution)/shard_map/gather_gx/pallas_call | solution.py:114
  13.6 24.0 %smooth.1 = (f32[64,72,512]{2,1,0:T(8,128)}, f32[4,2,72,128]{3,2,1,0:T(8,128)}) custom-call(bf16[512,512]{1,0:T(8,128)(2,1)} %bitcast.6, bf16[8,144,512]{2,1,0:T(8,128)(2,1)} %constant.8.clone.mx_ref, bf16[1,512,512]{2,1,0:T(8,128)(2,1)} %constant.9.clone.my_ref, bf16[512,512]{1,0:T(8,128)(2,1)} %constant.10.clone.spread_ref), custom_call_target="tpu_custom_call" | custom-call | tf_op jit(solution)/shard_map/smooth/pallas_call | solution.py:256
  37.6 30.4 %redistance.1 = f32[64,64,512]{2,1,0:T(8,128)} custom-call(f32[4,2,72,128]{3,2,1,0:T(8,128)} %get-tuple-element.7.tops_ref, f32[64,72,512]{2,1,0:T(8,128)} %get-tuple-element.8.u_ref, bf16[512,512]{1,0:T(8,128)(2,1)} %constant.11.clone.back_ref), custom_call_target="tpu_custom_call" | custom-call | tf_op jit(solution)/shard_map/redistance/pallas_call | solution.py:357

commit v7 on v4

--- a/solution.py
+++ b/solution.py
@@ -122,13 +122,20 @@
     )(labels, table)
 
 
-def merge_kernel(axis, size, x_ref, out_ref, recv_ref, send_sem, recv_sem, back_send, back_recv):
+def peers(axis, size):
     me = lax.axis_index(axis)
-    others = [lax.rem(me + k, size) for k in range(1, size)]
+    return me, [lax.rem(me + k, size) for k in range(1, size)]
+
+
+def greet(axis, size):
     barrier = pltpu.get_barrier_semaphore()
-    for device in others:
+    for device in peers(axis, size)[1]:
         pl.semaphore_signal(barrier, inc=1, device_id={axis: device}, device_id_type=MESH)
-    pl.semaphore_wait(barrier, size - 1)
+
+
+def merge(axis, size, x_ref, out_ref, recv_ref, send_sem, recv_sem, back_send, back_recv):
+    me, others = peers(axis, size)
+    pl.semaphore_wait(pltpu.get_barrier_semaphore(), size - 1)
 
     def send(src, dst, sems, k, device):
         copy = pltpu.make_async_remote_copy(
@@ -164,21 +171,6 @@
         copy.wait()
 
 
-def merged(x, axis, size, collective_id):
-    return pl.pallas_call(
-        functools.partial(merge_kernel, axis, size),
-        out_shape=jax.ShapeDtypeStruct(x.shape, x.dtype),
-        in_specs=[pl.BlockSpec(memory_space=pltpu.VMEM)],
-        out_specs=pl.BlockSpec(memory_space=pltpu.VMEM),
-        scratch_shapes=[pltpu.VMEM((size - 1, *x.shape[1:]), x.dtype)]
-        + [pltpu.SemaphoreType.DMA((size - 1,))] * 4,
-        compiler_params=pltpu.CompilerParams(
-            collective_id=collective_id, has_side_effects=True, vmem_limit_bytes=VMEM
-        ),
-        name="merge_" + axis,
-    )(x)
-
-
 def tile_place(k, per_piece):
     row = 8 * (k % per_piece)
     return k // per_piece, slice(row, row + 8)
@@ -186,7 +178,7 @@
 
 def smooth_kernel(
     x_local, fam_local, group,
-    owner_ref, mx_ref, my_ref, u_ref, tops_ref, rel_ref, own_ref, t_ref,
+    owner_ref, mx_ref, my_ref, u_ref, all_ref, rel_ref, own_ref, t_ref, tops_ref, *exchange,
 ):
     step = pl.program_id(0)
     nx, ny = owner_ref.shape
@@ -196,6 +188,7 @@
 
     @pl.when(step == 0)
     def _():
+        greet("fam", tops_ref.shape[0])
         mine = owner_ref[pl.ds(pl.multiple_of(x0, x_local), x_local), :].astype(jnp.float32)
         after = lax.rem(x0 + x_local, nx)
         before = lax.rem(x0 + nx - 16, nx)
@@ -238,6 +231,11 @@
             tops_ref[piece, 0, place, :] = high
             tops_ref[piece, 1, place, :] = second
 
+    @pl.when(step == pl.num_programs(0) - 1)
+    def _():
+        merge("fam", tops_ref.shape[0], tops_ref, *exchange)
+        all_ref[...] = exchange[0][...]
+
 
 def smoothed(owner, mx, my, x_local, fam_local, fams):
     nx, ny = owner.shape
@@ -265,14 +263,20 @@
             pltpu.VMEM((nx, ny), jnp.bfloat16),
             pltpu.VMEM((rows, ny), jnp.float32),
             pltpu.VMEM((group * rows, ny), jnp.float32),
-        ],
-        compiler_params=pltpu.CompilerParams(vmem_limit_bytes=VMEM),
+            pltpu.VMEM(pieces, jnp.float32),
+            pltpu.VMEM(pieces, jnp.float32),
+            pltpu.VMEM((fams - 1, *pieces[1:]), jnp.float32),
+        ]
+        + [pltpu.SemaphoreType.DMA((fams - 1,))] * 4,
+        compiler_params=pltpu.CompilerParams(
+            collective_id=1, has_side_effects=True, vmem_limit_bytes=VMEM
+        ),
         name="smooth",
     )(owner, mx, my)
 
 
 def redistance_kernel(
-    x_local, group, tops_ref, u_ref, out_ref, half_ref, first_ref, phi_ref, flag_ref
+    x_local, group, tops_ref, u_ref, out_ref, half_ref, first_ref, phi_ref
 ):
     rows, ny = u_ref.shape[1:]
     chunks = ny // LANES
@@ -301,8 +305,15 @@
                 put(first_ref.at[j], r, c, phi)
                 half_ref[j, strip(r), chunk(c)] = phi * (step_size * lax.rsqrt(phi * phi + 1.0))
                 peaks[j] = jnp.maximum(peaks[j], phi)
+    family = lax.broadcasted_iota(jnp.int32, (8, LANES), 0)
+    peak = jnp.full((8, LANES), BIG, jnp.float32)
     for j in range(group):
-        flag_ref[j] = (jnp.max(peaks[j]) > 0.0).astype(jnp.int32)
+        highest = jnp.max(peaks[j], axis=0, keepdims=True)
+        peak = jnp.where(family == j, jnp.broadcast_to(highest, peak.shape), peak)
+    bit = lax.shift_left(jnp.ones_like(family), family).astype(jnp.float32)
+    peak = jnp.broadcast_to(jnp.max(peak, axis=1, keepdims=True), peak.shape)
+    some = jnp.sum(jnp.where(peak > 0.0, bit, 0.0), axis=0, keepdims=True)
+    flags = jnp.max(some).astype(jnp.int32)
 
     lane = lax.broadcasted_iota(jnp.int32, (8, LANES), 1)
     is_first, is_last = lane == 0, lane == LANES - 1
@@ -349,11 +360,13 @@
                         put(dst, r, c, new)
 
     def one(j, carry):
-        @pl.when(flag_ref[j] == 0)
+        flag = lax.bitwise_and(lax.shift_right_logical(flags, j), 1)
+
+        @pl.when(flag == 0)
         def _():
             sweeps(j, False)
 
-        @pl.when(flag_ref[j] != 0)
+        @pl.when(flag != 0)
         def _():
             sweeps(j, True)
 
@@ -379,7 +392,6 @@
             pltpu.VMEM((group, rows, ny), jnp.float32),
             pltpu.VMEM((group, chunks, rows + HALO, LANES), jnp.float32),
             pltpu.VMEM((2, chunks, rows + HALO, LANES), jnp.float32),
-            pltpu.SMEM((group,), jnp.int32),
         ],
         compiler_params=pltpu.CompilerParams(vmem_limit_bytes=VMEM),
         name="redistance",
@@ -395,7 +407,6 @@
     table = family_of_grain.reshape(-1, LANES)
     owner = gathered_owners(labels[0], table, "gx", parts, 0).reshape(nx, ny)
     u, tops = smoothed(owner, mx, my, x_local, fam_local, fams)
-    tops = merged(tops, "fam", fams, 1)
     return redistanced(tops, u, x_local)[:, None]
 
 

time: 71.1 us -> 68.5 us (0.963)
  Pallas kernels: 70.8 us -> 68.2 us
    pallas_call x1 -> x0, Pallas kernels: 14.4 us -> none  [merged(): pl.pallas_call(functools.partial(merge_kernel, axis, size), out_shape=jax...]
    pallas_call x1, Pallas kernels: 12.2 us -> 23.7 us  [smoothed(): pl.pallas_call(functools.partial(smooth_kernel, x_local, fam_local, group...]
where the time goes in v7:
time: 68.5 us; the launch traced here: 68.2 us
  Pallas kernels  68.2 us (100%)
    pallas_call x1, Pallas kernels, redistanced(): pl.pallas_call(functools.partial(redistance_kernel, x_local, group), grid...  31 us
    pallas_call x1, Pallas kernels, smoothed(): pl.pallas_call(functools.partial(smooth_kernel, x_local, fam_local, group...  23.7 us
    pallas_call x1, Pallas kernels, gathered_owners(): pl.pallas_call(functools.partial(gather_kernel, axis, size), out_shape=ja...  13.6 us

profile of v7, /device:TPU:0, one launch (start us, length us, event | category | flops | bytes accessed | tf_op | source)
XLA Modules:
  0.0 68.2 jit_solution(11650870844212305606)
XLA Ops:
  0.0 13.6 %gather_gx.1 = bf16[8,64,512]{2,1,0:T(8,128)(2,1)} custom-call(s32[64,512]{1,0:T(8,128)} %bitcast.7, s32[16,128]{1,0:T(8,128)} %bitcast.8), custom_call_target="tpu_custom_call" | custom-call | tf_op jit(solution)/shard_map/gather_gx/pallas_call | solution.py:107
  13.6 23.7 %smooth.1 = (f32[64,72,512]{2,1,0:T(8,128)}, f32[4,2,72,128]{3,2,1,0:T(8,128)}) custom-call(bf16[512,512]{1,0:T(8,128)(2,1)} %bitcast.6, bf16[8,144,512]{2,1,0:T(8,128)(2,1)} %constant.4.clone.mx_ref, bf16[1,512,512]{2,1,0:T(8,128)(2,1)} %constant.5.clone.my_ref), custom_call_target="tpu_custom_call" | custom-call | tf_op jit(solution)/shard_map/smooth/pallas_call | solution.py:246
  37.2 31.0 %redistance.1 = f32[64,64,512]{2,1,0:T(8,128)} custom-call(f32[4,2,72,128]{3,2,1,0:T(8,128)} %get-tuple-element.7.tops_ref, f32[64,72,512]{2,1,0:T(8,128)} %get-tuple-element.8.u_ref), custom_call_target="tpu_custom_call" | custom-call | tf_op jit(solution)/shard_map/redistance/pallas_call | solution.py:382

commit v8 on v5

--- a/solution.py
+++ b/solution.py
@@ -275,7 +275,7 @@
     )(owner, mx, my)
 
 
-def redistance_kernel(x_local, group, tops_ref, u_ref, out_ref, phi_ref, sig_ref, half_ref):
+def redistance_kernel(x_local, group, lanes, tops_ref, u_ref, out_ref, *scratch):
     rows, ny = u_ref.shape[1:]
     chunks = ny // LANES
     strips = rows // 8
@@ -284,12 +284,16 @@
     lane = lax.broadcasted_iota(jnp.int32, (8, LANES), 1)
     is_first, is_last = lane == 0, lane == LANES - 1
 
-    def put(slot, r, c, value):
-        phi_ref[slot, c, 8 * r + HALO : 8 * r + HALO + 8, :] = value
+    phis = [scratch[4 * p : 4 * p + 2] for p in range(lanes)]
+    sigs = [scratch[4 * p + 2] for p in range(lanes)]
+    halves = [scratch[4 * p + 3] for p in range(lanes)]
+
+    def put(ref, r, c, value):
+        ref[c, 8 * r + HALO : 8 * r + HALO + 8, :] = value
         if r == strips - 1:
-            phi_ref[slot, c, 0:HALO, :] = value
-
-    def one(j, carry):
+            ref[c, 0:HALO, :] = value
+
+    def start(j, p):
         for r in range(strips):
             for c in range(chunks):
                 rs, cs = slice(8 * r, 8 * r + 8), slice(c * LANES, (c + 1) * LANES)
@@ -297,47 +301,56 @@
                 piece, place = tile_place(r * chunks + c, per_piece)
                 top1, top2 = tops_ref[piece, 0, place, :], tops_ref[piece, 1, place, :]
                 phi = scale_factor * (u - jnp.where(u >= top1, top2, top1))
-                put(0, r, c, phi)
-                sig_ref[c, rs, :] = jnp.where(phi > 0.0, 1.0, -1.0)
-                half_ref[c, rs, :] = phi * (step_size * lax.rsqrt(phi * phi + 1.0))
+                put(phis[p][0], r, c, phi)
+                sigs[p][c, rs, :] = jnp.where(phi > 0.0, 1.0, -1.0)
+                halves[p][c, rs, :] = phi * (step_size * lax.rsqrt(phi * phi + 1.0))
+
+    def sweep_once(j, p, sweep):
+        src, dst = phis[p][sweep % 2], phis[p][(sweep + 1) % 2]
+        final = sweep == SWEEPS - 1
+        for r in range(x_local // 8 if final else strips):
+            rs = slice(8 * r, 8 * r + 8)
+            mid = [src[c, 8 * r + HALO : 8 * r + HALO + 8, :] for c in range(chunks)]
+            to_right = [pltpu.roll(v, 1, 1) for v in mid]
+            to_left = [pltpu.roll(v, LANES - 1, 1) for v in mid]
+            for c in range(chunks):
+                sig, half, centre = sigs[p][c, rs, :], halves[p][c, rs, :], mid[c]
+                y_low = jnp.where(is_first, to_right[c - 1], to_right[c])
+                y_high = jnp.where(is_last, to_left[(c + 1) % chunks], to_left[c])
+                x_low = src[c, 8 * r + HALO - 1 : 8 * r + HALO + 7, :]
+                if r == strips - 1:
+                    x_high = src[c, 1:9, :]
+                else:
+                    x_high = src[c, 8 * r + HALO + 1 : 8 * r + HALO + 9, :]
+                here = centre * sig
+                gx = jnp.maximum(here - jnp.minimum(x_low * sig, x_high * sig), 1e-18)
+                gy = jnp.maximum(here - jnp.minimum(y_low * sig, y_high * sig), 1e-18)
+                square = gx * gx + gy * gy
+                grad = square * lax.rsqrt(square)
+                new = centre - half * (grad - 1.0)
+                if final:
+                    out_ref[j, rs, c * LANES : (c + 1) * LANES] = new
+                else:
+                    put(dst, r, c, new)
+
+    def some(i, carry):
+        for p in range(lanes):
+            start(i * lanes + p, p)
         for sweep in range(SWEEPS):
-            src, dst = sweep % 2, (sweep + 1) % 2
-            final = sweep == SWEEPS - 1
-            for r in range(x_local // 8 if final else strips):
-                rs = slice(8 * r, 8 * r + 8)
-                mid = [phi_ref[src, c, 8 * r + HALO : 8 * r + HALO + 8, :] for c in range(chunks)]
-                to_right = [pltpu.roll(v, 1, 1) for v in mid]
-                to_left = [pltpu.roll(v, LANES - 1, 1) for v in mid]
-                for c in range(chunks):
-                    sig, half, centre = sig_ref[c, rs, :], half_ref[c, rs, :], mid[c]
-                    y_low = jnp.where(is_first, to_right[c - 1], to_right[c])
-                    y_high = jnp.where(is_last, to_left[(c + 1) % chunks], to_left[c])
-                    x_low = phi_ref[src, c, 8 * r + HALO - 1 : 8 * r + HALO + 7, :]
-                    if r == strips - 1:
-                        x_high = phi_ref[src, c, 1:9, :]
-                    else:
-                        x_high = phi_ref[src, c, 8 * r + HALO + 1 : 8 * r + HALO + 9, :]
-                    here = centre * sig
-                    gx = jnp.maximum(here - jnp.minimum(x_low * sig, x_high * sig), 1e-18)
-                    gy = jnp.maximum(here - jnp.minimum(y_low * sig, y_high * sig), 1e-18)
-                    square = gx * gx + gy * gy
-                    grad = square * lax.rsqrt(square)
-                    new = centre - half * (grad - 1.0)
-                    if final:
-                        out_ref[j, rs, c * LANES : (c + 1) * LANES] = new
-                    else:
-                        put(dst, r, c, new)
+            for p in range(lanes):
+                sweep_once(i * lanes + p, p, sweep)
         return carry
 
-    lax.fori_loop(0, group, one, 0)
+    lax.fori_loop(0, group // lanes, some, 0)
 
 
 def redistanced(tops, u, x_local):
     fam_local, rows, ny = u.shape
     group = min(8, fam_local)
+    lanes = 4 if group % 4 == 0 else 1
     chunks = ny // LANES
     return pl.pallas_call(
-        functools.partial(redistance_kernel, x_local, group),
+        functools.partial(redistance_kernel, x_local, group, lanes),
         grid=(fam_local // group,),
         out_shape=jax.ShapeDtypeStruct((fam_local, x_local, ny), jnp.float32),
         in_specs=[
@@ -346,10 +359,12 @@
         ],
         out_specs=pl.BlockSpec((group, x_local, ny), lambda i: (i, 0, 0)),
         scratch_shapes=[
-            pltpu.VMEM((2, chunks, rows + HALO, LANES), jnp.float32),
+            pltpu.VMEM((chunks, rows + HALO, LANES), jnp.float32),
+            pltpu.VMEM((chunks, rows + HALO, LANES), jnp.float32),
             pltpu.VMEM((chunks, rows, LANES), jnp.float32),
             pltpu.VMEM((chunks, rows, LANES), jnp.float32),
-        ],
+        ]
+        * lanes,
         compiler_params=pltpu.CompilerParams(vmem_limit_bytes=VMEM),
         name="redistance",
     )(tops, u)

time: 64.3 us -> 62.8 us (0.977)
  Pallas kernels: 64.1 us -> 62.6 us
    pallas_call x1, Pallas kernels: 26.9 us -> 25.4 us  [redistanced(): pl.pallas_call(functools.partial(redistance_kernel, x_local, group, lanes...]
where the time goes in v8:
time: 62.8 us; the launch traced here: 62.7 us
  Pallas kernels  62.6 us (100%)
    pallas_call x1, Pallas kernels, redistanced(): pl.pallas_call(functools.partial(redistance_kernel, x_local, group, lanes...  25.4 us
    pallas_call x1, Pallas kernels, smoothed(): pl.pallas_call(functools.partial(smooth_kernel, x_local, fam_local, group...  23.7 us
    pallas_call x1, Pallas kernels, gathered_owners(): pl.pallas_call(functools.partial(gather_kernel, axis, size), out_shape=ja...  13.6 us

profile of v8, /device:TPU:0, one launch (start us, length us, event | category | flops | bytes accessed | tf_op | source)
XLA Modules:
  0.0 62.7 jit_solution(7726838070355746936)
XLA Ops:
  0.0 13.6 %gather_gx.1 = bf16[8,64,512]{2,1,0:T(8,128)(2,1)} custom-call(s32[64,512]{1,0:T(8,128)} %bitcast.7, s32[16,128]{1,0:T(8,128)} %bitcast.8), custom_call_target="tpu_custom_call" | custom-call | tf_op jit(solution)/shard_map/gather_gx/pallas_call | solution.py:107
  13.6 23.7 %smooth.1 = (f32[64,72,512]{2,1,0:T(8,128)}, f32[4,2,72,128]{3,2,1,0:T(8,128)}) custom-call(bf16[512,512]{1,0:T(8,128)(2,1)} %bitcast.6, bf16[8,144,512]{2,1,0:T(8,128)(2,1)} %constant.4.clone.mx_ref, bf16[1,512,512]{2,1,0:T(8,128)(2,1)} %constant.5.clone.my_ref), custom_call_target="tpu_custom_call" | custom-call | tf_op jit(solution)/shard_map/smooth/pallas_call | solution.py:246
  37.2 25.4 %redistance.1 = f32[64,64,512]{2,1,0:T(8,128)} custom-call(f32[4,2,72,128]{3,2,1,0:T(8,128)} %get-tuple-element.7.tops_ref, f32[64,72,512]{2,1,0:T(8,128)} %get-tuple-element.8.u_ref), custom_call_target="tpu_custom_call" | custom-call | tf_op jit(solution)/shard_map/redistance/pallas_call | solution.py:352
